TPU v7x, 256 devices: a whole 4x4x8 slice. The times are simulated.
256 devices in a mesh: row: 16 (over y, x), col: 16 (over z, core).
Axes of the slice: x: 4, y: 4, z: 8, core: 2. Of those that a mesh axis runs over, the one named last changes fastest.
Arguments:
- leaf_state_map: bfloat16 [1024, 512, 512], P(('row', 'col')), may hold values from -0.1875 to 0.1875
- leaf_input_map: bfloat16 [1024, 512, 256], P(('row', 'col')), may hold values from -0.25 to 0.25
- leaf_weight: bfloat16 [1024], P(('row', 'col')), may hold values from 0.29882812 to 3
- leaf_count: int32 [256], P(('row', 'col')), may hold values from 1 to 4, as said below
- mid_state_map: bfloat16 [256, 512, 512], P(('row', 'col')), may hold values from -0.1875 to 0.1875
- mid_input_map: bfloat16 [256, 512, 256], P(('row', 'col')), may hold values from -0.25 to 0.25
- mid_weight: float32 [256], P(('row', 'col')), may hold values from 0.3 to 3
- mid_parent: int32 [256], P(('row', 'col')), may hold values from 0 to 1, as said below
- up_state_map: bfloat16 [32, 512, 512], P('row'), may hold values from -0.1875 to 0.1875
- up_input_map: bfloat16 [32, 512, 256], P('row'), may hold values from -0.25 to 0.25
- up_weight: float32 [32], P('row'), may hold values from 0.3 to 3
- root_cov: bfloat16 [512, 512], replicated, as said below
- state_cost: float32 [512], replicated, may hold values from 0.3 to 3
- control_cost: float32 [256], replicated, may hold values from 0.3 to 3
- noise_cov: float32 [512], replicated, may hold values from 0.05 to 0.5
Outputs:
- root_gain: bfloat16 [256, 512], replicated
- root_value: bfloat16 [512, 512], replicated
- up_gain: bfloat16 [32, 256, 512], P('row')
- up_value: bfloat16 [32, 512, 512], P('row')
- up_cov: bfloat16 [32, 512, 512], P('row')
- mid_gain: bfloat16 [256, 256, 512], P(('row', 'col'))
- mid_value: bfloat16 [256, 512, 512], P(('row', 'col'))
- mid_cov: bfloat16 [256, 512, 512], P(('row', 'col'))
- leaf_cov: bfloat16 [1024, 512, 512], P(('row', 'col'))
Inputs may be any that keep to these rules, and one draw needn't show every extreme that they name: `leaf_count`: the number of live leaves of each section-2 node; some node has 4 in every draw. `mid_parent`: the parent slot of each section-2 node within its row group; every section-1 node has at least one child. `root_cov`: symmetric positive definite.
All inputs are finite; a program needn't handle non-finite values.
Results may differ from a plain program's by a relative error of at most 0.02.
Values may be sent and summed in bfloat16 or wider, within the bound.
A program may use at most 128 MiB of HBM per device.

v0:
```python
import jax
import jax.numpy as jnp
from jax import lax
from jax.sharding import PartitionSpec as P

NX = 512
NU = 256
S1_ROW = 2


exact_mode = lax.Precision.HIGHEST


def contract(joined, applied):
    return lax.dot_general(
        joined, applied, (((0,), (0,)), ((), ())), preferred_element_type=jnp.float32
    )


def pack_flat(members):
    return jnp.concatenate([member.reshape(-1) for member in members])


def unpack_flat(flat, templates):
    result = []
    offset = 0
    for template in templates:
        amount = template.size
        result.append(flat[offset : offset + amount].reshape(template.shape))
        offset = offset + amount
    return result


def term_parts(joined, applied):
    return (contract(joined, applied),)


def empty_parts():
    return (jnp.zeros((NX + NU, NX + NU), jnp.float32),)


def leaf_parts(state_map, input_map, state_cost):
    joined = jnp.concatenate([state_map, input_map], axis=1)
    applied = (state_cost[:, None] * joined.astype(jnp.float32)).astype(jnp.bfloat16)
    return term_parts(joined, applied)


def node_parts(value_matrix, state_map, input_map):
    joined = jnp.concatenate([state_map, input_map], axis=1)
    applied = jnp.dot(value_matrix, joined, preferred_element_type=jnp.float32).astype(jnp.bfloat16)
    return term_parts(joined, applied)


def riccati(parts, state_cost, control_cost):
    combined = parts[0]
    block_aa = combined[:NX, :NX]
    block_ba = combined[NX:, :NX]
    block_bb = combined[NX:, NX:]
    hessian = block_bb + jnp.diag(control_cost)
    factor = jnp.linalg.cholesky(hessian)
    feedback = -jax.scipy.linalg.cho_solve((factor, True), block_ba)
    value_matrix = (
        jnp.diag(state_cost) + block_aa + jnp.dot(block_ba.T, feedback, precision=exact_mode)
    )
    return (feedback.astype(jnp.bfloat16), value_matrix.astype(jnp.bfloat16))


def propagate(parent_cov, feedback, state_map, input_map, noise_cov):
    closed = (
        state_map.astype(jnp.float32)
        + jnp.dot(input_map, feedback, preferred_element_type=jnp.float32)
    ).astype(jnp.bfloat16)
    moved_cov = jnp.dot(closed, parent_cov, preferred_element_type=jnp.float32).astype(jnp.bfloat16)
    spread = lax.dot_general(
        moved_cov, closed, (((1,), (1,)), ((), ())), preferred_element_type=jnp.float32
    )
    return (spread + jnp.diag(noise_cov)).astype(jnp.bfloat16)


def local(
    leaf_state_map,
    leaf_input_map,
    leaf_weight,
    leaf_count,
    mid_state_map,
    mid_input_map,
    mid_weight,
    mid_parent,
    up_state_map,
    up_input_map,
    up_weight,
    root_cov,
    state_cost,
    control_cost,
    noise_cov,
):
    live_count = leaf_count[0]
    slot_total = leaf_state_map.shape[0]
    zero_weight = jnp.zeros((), jnp.float32)

    def add_leaf(leaf_index, running):
        parts_sum, weight_sum = running
        leaf_w = leaf_weight[leaf_index].astype(jnp.float32)
        fresh_parts = leaf_parts(leaf_state_map[leaf_index], leaf_input_map[leaf_index], state_cost)
        parts_sum = jax.tree.map(
            lambda old_part, new_part: old_part + leaf_w * new_part, parts_sum, fresh_parts
        )
        return (parts_sum, weight_sum + leaf_w)

    child_sum, child_weight = lax.fori_loop(0, live_count, add_leaf, (empty_parts(), zero_weight))
    child_mean = jax.tree.map(lambda part_item: part_item / child_weight, tuple(child_sum))
    mid_gain, mid_value = riccati(child_mean, state_cost, control_cost)
    parent_slot = mid_parent[0]
    slot_weight = (jnp.arange(S1_ROW, dtype=jnp.int32) == parent_slot).astype(
        jnp.float32
    ) * mid_weight[0]
    mid_term = node_parts(mid_value, mid_state_map[0], mid_input_map[0])
    slotted = jax.tree.map(lambda part_item: slot_weight[:, None, None] * part_item[None], mid_term)
    group_members = list(slotted) + [slot_weight]
    group_flat = lax.psum(pack_flat(group_members).astype(jnp.bfloat16), "col").astype(jnp.float32)
    group_unpacked = unpack_flat(group_flat, group_members)
    group_sum = tuple(group_unpacked[:-1])
    group_weight = group_unpacked[-1]
    upper_gains = []
    upper_values = []
    root_sum = empty_parts()
    for slot_number in range(S1_ROW):
        slot_mean = jax.tree.map(
            lambda part_item: part_item[slot_number] / group_weight[slot_number], group_sum
        )
        upper_gain, upper_value = riccati(slot_mean, state_cost, control_cost)
        upper_gains.append(upper_gain)
        upper_values.append(upper_value)
        upper_term = node_parts(upper_value, up_state_map[slot_number], up_input_map[slot_number])
        root_sum = jax.tree.map(
            lambda old_part, new_part: old_part + up_weight[slot_number] * new_part,
            root_sum,
            upper_term,
        )
    top_members = list(root_sum) + [jnp.sum(up_weight)]
    top_flat = lax.psum(pack_flat(top_members).astype(jnp.bfloat16), "row").astype(jnp.float32)
    top_unpacked = unpack_flat(top_flat, top_members)
    top_sum = tuple(top_unpacked[:-1])
    top_weight = top_unpacked[-1]
    root_mean = jax.tree.map(lambda part_item: part_item / top_weight, top_sum)
    root_gain, root_value = riccati(root_mean, state_cost, control_cost)
    upper_covs = []
    for slot_number in range(S1_ROW):
        upper_covs.append(
            propagate(
                root_cov, root_gain, up_state_map[slot_number], up_input_map[slot_number], noise_cov
            )
        )
    up_cov = jnp.stack(upper_covs)
    up_gain = jnp.stack(upper_gains)
    up_value = jnp.stack(upper_values)
    mid_cov = propagate(
        up_cov[parent_slot], up_gain[parent_slot], mid_state_map[0], mid_input_map[0], noise_cov
    )
    empty_stack = jnp.zeros((slot_total, NX, NX), jnp.bfloat16)

    def cover_leaf(leaf_index, cov_stack):
        leaf_result = propagate(
            mid_cov, mid_gain, leaf_state_map[leaf_index], leaf_input_map[leaf_index], noise_cov
        )
        return lax.dynamic_update_index_in_dim(cov_stack, leaf_result, leaf_index, 0)

    leaf_cov = lax.fori_loop(0, live_count, cover_leaf, empty_stack)
    return (
        root_gain,
        root_value,
        up_gain,
        up_value,
        up_cov,
        mid_gain[None],
        mid_value[None],
        mid_cov[None],
        leaf_cov,
    )


def solution(mesh):
    return jax.shard_map(
        local,
        mesh=mesh,
        in_specs=(
            P(("row", "col"), None, None),
            P(("row", "col"), None, None),
            P(("row", "col")),
            P(("row", "col")),
            P(("row", "col"), None, None),
            P(("row", "col"), None, None),
            P(("row", "col")),
            P(("row", "col")),
            P("row", None, None),
            P("row", None, None),
            P("row"),
            P(),
            P(),
            P(),
            P(),
        ),
        out_specs=(
            P(),
            P(),
            P("row", None, None),
            P("row", None, None),
            P("row", None, None),
            P(("row", "col"), None, None),
            P(("row", "col"), None, None),
            P(("row", "col"), None, None),
            P(("row", "col"), None, None),
        ),
        check_vma=False,
    )
```

profile of v0, /device:TPU:26, one launch (start us, length us, event | category | flops | bytes accessed | tf_op | source)
XLA Modules:
  0.0 651.0 jit_solution(2781746258172542836)
XLA Ops:
  8.8 23.4 %while.30 = (s32[]{:T(128)}, f32[768,768]{1,0:T(8,128)S(1)}, f32[]{:T(128)}, s32[]{:T(128)}, bf16[4]{0:T(256)(128)(2,1)S(1)}, /*index=5*/bf16[4,512,512]{2,1,0:T...) while((s32[]{:T(128)}, f32[768,768]{1,0:T(8,128)S(1)}, ...), condition=%wide.region_1.0_spmd, body=%wide.region_0.0_spmd.sunk | while | flops 609091584 | bytes 7080123 | solution.py:110
  36.3 11.7 %cholesky.214 = f32[128,128]{1,0:T(8,128)S(1)} custom-call(f32[128,128]{1,0:T(8,128)S(1)} %cholesky.346), custom_call_target="Cholesky" | custom-call | tf_op jit(solution)/shard_map/jit(cholesky)/cholesky | solution.py:60
  48.1 9.8 %custom-call.19 = f32[1,128,128]{1,2,0:T(8,128)S(1)} custom-call(f32[1,128,128]{2,1,0:T(8,128)S(1)} %get-tuple-element.262), custom_call_target="InvertDiagBlocksLowerTriangular" | custom-call | tf_op jit(solution)/shard_map/jit(cholesky)/cholesky | solution.py:60
  58.4 11.7 %cholesky.231 = f32[128,128]{1,0:T(8,128)S(1)} custom-call(f32[128,128]{1,0:T(8,128)S(1)} %convolution_subtract_fusion.11), custom_call_target="Cholesky" | custom-call | tf_op jit(solution)/shard_map/jit(cholesky)/cholesky | solution.py:60
  72.2 4.0 while.32
  76.2 19.9 %custom-call.20 = f32[2,128,128]{1,2,0:T(8,128)S(1)} custom-call(f32[2,128,128]{2,1,0:T(8,128)S(1)} %get-tuple-element.127), custom_call_target="InvertDiagBlocksLowerTriangular" | custom-call | tf_op jit(solution)/shard_map/jit(_cho_solve)/triangular_solve | solution.py:61
  110.0 4.2 mul.55
  123.1 111.8 %all-reduce.4.cloned.1.call-done = bf16[1179650]{0:T(1024)(128)(2,1)} async-done(((bf16[1179650]{0:T(1024)(128)(2,1)}), bf16[1179650]{0:T(1024)(128)(2,1)}) %all-reduce.4.cloned.1.call-update) | async-done | bytes 2359316 | tf_op jit(solution)/shard_map/psum | solution.py:120
  238.1 3.0 slice_divide_fusion.1
  241.1 3.4 div.43
  248.4 10.9 %div.46 = f32[768,768]{1,0:T(8,128)} reshape(f32[589824]{0:T(1024)S(1)} %get-tuple-element.239) | data formatting | bytes 4718592 | tf_op jit(solution)/shard_map/div | solution.py:129
  270.8 11.7 %cholesky.248 = f32[128,128]{1,0:T(8,128)S(1)} custom-call(f32[128,128]{1,0:T(8,128)S(1)} %cholesky.349), custom_call_target="Cholesky" | custom-call | tf_op jit(solution)/shard_map/jit(cholesky)/cholesky | solution.py:60
  282.6 9.8 %custom-call.21 = f32[1,128,128]{1,2,0:T(8,128)S(1)} custom-call(f32[1,128,128]{2,1,0:T(8,128)S(1)} %get-tuple-element.258), custom_call_target="InvertDiagBlocksLowerTriangular" | custom-call | tf_op jit(solution)/shard_map/jit(cholesky)/cholesky | solution.py:60
  294.6 11.7 %cholesky.265 = f32[128,128]{1,0:T(8,128)S(1)} custom-call(f32[128,128]{1,0:T(8,128)S(1)} %convolution_subtract_fusion.10), custom_call_target="Cholesky" | custom-call | tf_op jit(solution)/shard_map/jit(cholesky)/cholesky | solution.py:60
  309.9 4.0 while.33
  313.9 20.1 %custom-call.22 = f32[2,128,128]{1,2,0:T(8,128)S(1)} custom-call(f32[2,128,128]{2,1,0:T(8,128)S(1)} %get-tuple-element.128), custom_call_target="InvertDiagBlocksLowerTriangular" | custom-call | tf_op jit(solution)/shard_map/jit(_cho_solve)/triangular_solve | solution.py:61
  343.3 11.7 %cholesky.282 = f32[128,128]{1,0:T(8,128)S(1)} custom-call(f32[128,128]{1,0:T(8,128)S(1)} %cholesky.352), custom_call_target="Cholesky" | custom-call | tf_op jit(solution)/shard_map/jit(cholesky)/cholesky | solution.py:60
  355.1 9.8 %custom-call.23 = f32[1,128,128]{1,2,0:T(8,128)S(1)} custom-call(f32[1,128,128]{2,1,0:T(8,128)S(1)} %get-tuple-element.254), custom_call_target="InvertDiagBlocksLowerTriangular" | custom-call | tf_op jit(solution)/shard_map/jit(cholesky)/cholesky | solution.py:60
  365.3 11.9 %cholesky.299 = f32[128,128]{1,0:T(8,128)S(1)} custom-call(f32[128,128]{1,0:T(8,128)S(1)} %convolution_subtract_fusion.9), custom_call_target="Cholesky" | custom-call | tf_op jit(solution)/shard_map/jit(cholesky)/cholesky | solution.py:60
  379.9 4.0 while.34
  383.9 19.7 %custom-call.24 = f32[2,128,128]{1,2,0:T(8,128)S(1)} custom-call(f32[2,128,128]{2,1,0:T(8,128)S(1)} %get-tuple-element.129), custom_call_target="InvertDiagBlocksLowerTriangular" | custom-call | tf_op jit(solution)/shard_map/jit(_cho_solve)/triangular_solve | solution.py:61
  407.9 3.0 fusion.24
  414.0 3.9 fusion.19
  417.8 5.4 add_convert_fusion
  435.4 89.0 %all-reduce.6.cloned.1.call-done = bf16[589825]{0:T(1024)(128)(2,1)} async-done(((bf16[589825]{0:T(1024)(128)(2,1)}), bf16[589825]{0:T(1024)(128)(2,1)}) %all-reduce.6.cloned.1.call-update) | async-done | bytes 1179666 | tf_op jit(solution)/shard_map/psum | solution.py:141
  539.1 11.7 %cholesky.316 = f32[128,128]{1,0:T(8,128)S(1)} custom-call(f32[128,128]{1,0:T(8,128)S(1)} %cholesky.355), custom_call_target="Cholesky" | custom-call | tf_op jit(solution)/shard_map/jit(cholesky)/cholesky | solution.py:60
  550.9 9.8 %custom-call.25 = f32[1,128,128]{1,2,0:T(8,128)S(1)} custom-call(f32[1,128,128]{2,1,0:T(8,128)S(1)} %get-tuple-element.250), custom_call_target="InvertDiagBlocksLowerTriangular" | custom-call | tf_op jit(solution)/shard_map/jit(cholesky)/cholesky | solution.py:60
  562.8 11.7 %cholesky.333 = f32[128,128]{1,0:T(8,128)S(1)} custom-call(f32[128,128]{1,0:T(8,128)S(1)} %convolution_subtract_fusion.8), custom_call_target="Cholesky" | custom-call | tf_op jit(solution)/shard_map/jit(cholesky)/cholesky | solution.py:60
  578.2 4.0 while.35
  582.8 20.7 %custom-call.26 = f32[2,128,128]{1,2,0:T(8,128)S(1)} custom-call(f32[2,128,128]{2,1,0:T(8,128)} %copy-done.30), custom_call_target="InvertDiagBlocksLowerTriangular" | custom-call | tf_op jit(solution)/shard_map/jit(_cho_solve)/triangular_solve | solution.py:61
  612.5 3.2 fusion.26
  628.6 15.1 %while.31 = (s32[]{:T(128)}, bf16[4,512,512]{2,1,0:T(8,128)(2,1)}, s32[]{:T(128)}, bf16[4,512,512]{2,1,0:T(8,128)(2,1)}, bf16[4,512,256]{2,1,0:T(8,128)(2,1)}, /...) while((s32[]{:T(128)}, bf16[4,512,512]{2,1,0:T(8,128)(2,1)}, ...), condition=%wide.region_10.13_spmd, body=%wide.region_9.12_spmd.sunk | while | flops 673185792 | bytes 3673243 | solution.py:168
  (260 shorter events, 165.6 us)
Async XLA Ops:
  7.2 610.6 %copy-start = (bf16[512,512]{1,0:T(8,128)(2,1)S(1)}, bf16[512,512]{1,0:T(8,128)(2,1)}, u32[]{:S(2)}) copy-start(bf16[512,512]{1,0:T(8,128)(2,1)} %param.33) | copy-start | bytes 1572868
  7.2 1.6 copy-start.35
  7.2 1.6 copy-start.31
  7.2 227.7 %all-reduce.4.cloned.1.call-start = ((), (), s32[]{:S(2)}) async-start(), calls=%async_computation | async-start | bytes 4722688 | tf_op jit(solution)/shard_map/psum | solution.py:120
  34.2 1.8 copy-start.32
  76.2 21.0 %copy-start.16 = (f32[256,256]{1,0:T(8,128)}, f32[256,256]{1,0:T(8,128)S(1)}, u32[]{:S(2)}) copy-start(f32[256,256]{1,0:T(8,128)S(1)} %get-tuple-element.628) | copy-start | bytes 786436
  99.6 8.6 %copy-start.2 = (f32[128,512]{1,0:T(8,128)}, f32[128,512]{1,0:T(8,128)S(1)}, u32[]{:S(2)}) copy-start(f32[128,512]{1,0:T(8,128)S(1)} %fusion.103) | copy-start | bytes 786436
  116.9 1.9 copy-start.21
  116.9 407.5 %all-reduce.6.cloned.1.call-start = ((), (), s32[]{:S(2)}) async-start(), calls=%async_computation.1 | async-start | bytes 2363392 | tf_op jit(solution)/shard_map/psum | solution.py:141
  118.8 3.0 copy-start.33
  261.0 4.7 copy-start.22
  307.0 1.9 copy-start.19
  313.9 22.8 %copy-start.18 = (f32[256,256]{1,0:T(8,128)}, f32[256,256]{1,0:T(8,128)S(1)}, u32[]{:S(2)}) copy-start(f32[256,256]{1,0:T(8,128)S(1)} %get-tuple-element.630) | copy-start | bytes 786436
  379.9 28.0 %copy-start.4 = (f32[128,512]{1,0:T(8,128)S(1)}, f32[128,512]{1,0:T(8,128)}, u32[]{:S(2)}) copy-start(f32[128,512]{1,0:T(8,128)} %fusion.106) | copy-start | bytes 786436
  406.7 4.3 copy-start.1
  407.9 6.0 copy-start.5
  407.9 6.0 copy-start.28
  411.0 3.0 copy-start.9
  414.0 3.9 copy-start.11
  414.0 3.9 copy-start.29
  425.9 3.9 copy-start.3
  430.5 2.7 copy-start.6
  431.8 2.3 copy-start.23
  575.2 1.9 copy-start.20
  582.8 21.6 %copy-start.17 = (f32[256,256]{1,0:T(8,128)}, f32[256,256]{1,0:T(8,128)S(1)}, u32[]{:S(2)}) copy-start(f32[256,256]{1,0:T(8,128)S(1)} %get-tuple-element.629) | copy-start | bytes 786436
  603.6 4.0 copy-start.12
  603.6 4.0 copy-start.14
  604.4 4.4 copy-start.10
  607.6 1.2 copy-start.8
  612.5 5.3 copy-start.34
  615.7 4.2 copy-start.26
  621.5 2.5 copy-start.27
  (6 other events, 4.9 us)
Sparse Core Ops, SparseCore 0:
  117.1 117.8 all-reduce.3
  427.8 96.5 all-reduce.5
where the time goes:
time: 664 us; the launch traced here: 651 us
  other arithmetic  247 us (37%)
  waiting for transfers between devices  201 us (30%)
  local copies, waits for them, and re-layouts  98.5 us (15%)
  matrix products  70.2 us (11%)
  between operations  22 us (3%)
  loops' own time  12.1 us (2%)
    another operation x27, other arithmetic, riccati(): factor = jnp.linalg.cholesky(hessian)  138 us
    psum x1, waiting for transfers between devices, local(): lax.psum(pack_flat(group_members).astype(jnp.bfloat16), 'col')  112 us
    psum x1, waiting for transfers between devices, local(): lax.psum(pack_flat(top_members).astype(jnp.bfloat16), 'row')  89 us
    another operation x9, other arithmetic, riccati(): feedback = -jax.scipy.linalg.cho_solve((factor, True), block_ba)  82.4 us
    unnamed x89, local copies, waits for them, and re-layouts  28.5 us
    another operation x24, matrix products, riccati(): feedback = -jax.scipy.linalg.cho_solve((factor, True), block_ba)  16.7 us
    dot_general x7, matrix products, contract(): lax.dot_general(joined, applied, (((0,), (0,)), ((), ())), preferred_elem...  16.4 us
    another operation x29, local copies, waits for them, and re-layouts, riccati(): feedback = -jax.scipy.linalg.cho_solve((factor, True), block_ba)  15.9 us
  transfers between devices with their start and end apart: 2, of which 2 were waited for; matrix products, arithmetic and copies ran while one was open for 2% of the time, Pallas kernels for 0%

commit v1 on v0

v1 whole, which is shorter than its diff:
```python
import functools

import jax
import jax.numpy as jnp
from jax import lax
from jax.experimental import pallas as pl
from jax.experimental.pallas import tpu as pltpu
from jax.sharding import PartitionSpec as P

NX = 512
NU = 256
H = 256
LEAF = 4
ROWS = 6 * H
BLOCKS = ((0, 0), (1, 0), (1, 1), (2, 0), (2, 1), (2, 2))
F32 = jnp.float32
BF16 = jnp.bfloat16
MESH = pl.DeviceIdType.MESH
VMEM_LIMIT = 56 * 1024 * 1024
N_CHUNK = 16
CHUNK = ROWS // N_CHUNK
N_GV = 12
GV_ROWS = NX + NU
GV_CHUNK = GV_ROWS // N_GV
PIECE = ROWS // 16
HALF = PIECE // 2
REFINE_TOL = 1e-6
MAX_REFINE = 8


def mm(a, b):
    return jnp.dot(a, b, preferred_element_type=F32)


def mm_tn(a, b):
    return lax.dot_general(a, b, (((0,), (0,)), ((), ())), preferred_element_type=F32)


def mm_nt(a, b):
    return lax.dot_general(a, b, (((1,), (1,)), ((), ())), preferred_element_type=F32)


def split(a):
    hi = a.astype(BF16)
    return hi, (a - hi.astype(F32)).astype(BF16)


def iota2(shape, dim):
    return lax.broadcasted_iota(jnp.int32, shape, dim)


def eye_mask(n):
    return iota2((n, n), 0) == iota2((n, n), 1)


def to_column(row):
    n = row.shape[1]
    parts = []
    for i in range(n // 128):
        block = jnp.broadcast_to(row[:, i * 128 : (i + 1) * 128], (128, 128))
        parts.append(jnp.sum(jnp.where(eye_mask(128), block, 0.0), axis=1, keepdims=True))
    return jnp.concatenate(parts, axis=0)


def add_diag(block, row):
    return block + jnp.where(eye_mask(block.shape[0]), row, 0.0)


def all_sum(a):
    return jnp.sum(jnp.sum(a, axis=1, keepdims=True), axis=0, keepdims=True)


def riccati(get, state_row, control_row, gain_ref, value_ref, work, feed):
    hess = add_diag(get(5), control_row)
    ba = jnp.concatenate([get(3), get(4)], axis=1)
    eye = eye_mask(H)
    upper = jnp.max(jnp.max(jnp.sum(jnp.abs(hess), axis=1, keepdims=True), axis=0, keepdims=True))
    lower = jnp.minimum(jnp.min(control_row), upper)
    mid = 0.5 * (upper + lower)
    rad = 0.5 * (upper - lower)
    den = 2.0 * mid * mid - rad * rad
    error0 = rad * rad / den
    steps = jnp.int32(0)
    for j in range(16):
        steps += (error0 > 0.1 ** (0.5**j)).astype(jnp.int32)
    h_hi, h_lo = split(hess)
    ba_hi, ba_lo = split(ba)
    work[...] = jnp.where(eye, 4.0 * mid / den, 0.0) - (2.0 / den) * hess

    def newton(_, carry):
        x = work[...]
        x_hi = x.astype(BF16)
        res = jnp.where(eye, 1.0, 0.0) - mm(h_hi, x_hi)
        work[...] = x + mm(x_hi, res.astype(BF16))
        return carry

    lax.fori_loop(0, steps, newton, 0)
    inv = work[...].astype(BF16)
    feed[...] = -mm(inv, ba_hi)

    def unconverged(state):
        count, done = state
        return jnp.logical_and(count < MAX_REFINE, done == 0)

    def refine(state):
        count, _ = state
        f = feed[...]
        f_hi, f_lo = split(f)
        res = ba + (mm(h_hi, f_hi) + (mm(h_hi, f_lo) + mm(h_lo, f_hi)))
        step = mm(inv, res.astype(BF16))
        new = f - step
        feed[...] = new
        small = jnp.sum(step * step) <= REFINE_TOL * jnp.sum(new * new)
        return count + 1, small.astype(jnp.int32)

    _, done = lax.while_loop(unconverged, refine, (jnp.int32(0), jnp.int32(0)))

    @pl.when(done == 0)
    def _():
        work[...] = hess

        def sweep(k, carry):
            a = work[...]
            row = work[pl.ds(k, 1), :]
            here = iota2((H, H), 1) == k
            col = jnp.sum(jnp.where(here, a, 0.0), axis=1, keepdims=True)
            lane_k = iota2((1, H), 1) == k
            sub_k = iota2((H, 1), 0) == k
            pivot = jnp.sum(jnp.where(lane_k, row, 0.0), axis=1, keepdims=True)
            inv_p = 1.0 / pivot
            col0 = jnp.where(sub_k, 0.0, col)
            row1 = jnp.where(lane_k, 1.0, row) * inv_p
            base = jnp.where(jnp.logical_or(here, sub_k), 0.0, a)
            work[...] = jnp.where(sub_k, row1, base - col0 * row1)
            return carry

        lax.fori_loop(0, H, sweep, 0)
        feed[...] = -jnp.dot(
            work[...], ba, preferred_element_type=F32, precision=lax.Precision.HIGHEST
        )

    f = feed[...]
    f_hi, f_lo = split(f)
    gain_ref[...] = f_hi

    def quad(i, j):
        a = slice(i * H, (i + 1) * H)
        b = slice(j * H, (j + 1) * H)
        return mm_tn(ba_hi[:, a], f_hi[:, b]) + (
            mm_tn(ba_hi[:, a], f_lo[:, b]) + mm_tn(ba_lo[:, a], f_hi[:, b])
        )

    value_ref[:H, :H] = add_diag(get(0) + quad(0, 0), state_row[:, :H]).astype(BF16)
    cross = get(1) + quad(1, 0)
    value_ref[H:, :H] = cross.astype(BF16)
    value_ref[:H, H:] = cross.T.astype(BF16)
    value_ref[H:, H:] = add_diag(get(2) + quad(1, 1), state_row[:, H:]).astype(BF16)


def node_term(value_ref, state_ref, input_ref, put):
    value = value_ref[...]
    xs = [state_ref[:, :H], state_ref[:, H:], input_ref[...]]
    ys = [mm(value, x).astype(BF16) for x in xs]
    for i, (a, b) in enumerate(BLOCKS):
        put(i, mm_tn(xs[a], ys[b]))


def propagate(cov, gain, state, inputs, noise_row):
    closed = (state.astype(F32) + mm(inputs, gain)).astype(BF16)
    moved = mm(closed, cov).astype(BF16)
    top = mm_nt(moved[:H], closed[:H])
    cross = mm_nt(moved[H:], closed[:H])
    low = mm_nt(moved[H:], closed[H:])
    return (
        add_diag(top, noise_row[:, :H]).astype(BF16),
        cross.astype(BF16),
        cross.T.astype(BF16),
        add_diag(low, noise_row[:, H:]).astype(BF16),
    )


def store_cov(ref, blocks):
    ref[:H, :H] = blocks[0]
    ref[H:, :H] = blocks[1]
    ref[:H, H:] = blocks[2]
    ref[H:, H:] = blocks[3]


def lane(row, k):
    return jnp.sum(jnp.where(iota2(row.shape, 1) == k, row, 0.0), axis=1, keepdims=True)


def lower_kernel(
    count_ref, parent_ref, midw_ref, leaf_s, leaf_u, mid_s, mid_u, leafw_ref, sc_ref, cc_ref,
    gain_ref, value_ref, own_ref, other_ref, tile_ref,
    ls, lu, ms, mu, total, work, feed, sems,
):
    copies = []
    for c in range(LEAF):
        copies.append(pltpu.make_async_copy(leaf_s.at[c], ls.at[pl.ds(c * NX, NX)], sems.at[2 * c]))
        copies.append(pltpu.make_async_copy(leaf_u.at[c], lu.at[pl.ds(c * NX, NX)], sems.at[2 * c + 1]))
    copies.append(pltpu.make_async_copy(mid_s.at[0], ms, sems.at[2 * LEAF]))
    copies.append(pltpu.make_async_copy(mid_u.at[0], mu, sems.at[2 * LEAF + 1]))
    for copy in copies:
        copy.start()
    live = count_ref[0]
    weights = leafw_ref[...].astype(F32)
    weights = jnp.where(iota2(weights.shape, 1) < live, weights, 0.0)
    weights = weights / jnp.sum(weights, axis=1, keepdims=True)
    cost = to_column(sc_ref[...])
    for c in range(LEAF):
        copies[2 * c].wait()
        copies[2 * c + 1].wait()
        scale = cost * lane(weights, c)
        rows = slice(c * NX, (c + 1) * NX)
        xs = [ls[rows, :H], ls[rows, H:], lu[rows, :]]
        ss = [(scale * x.astype(F32)).astype(BF16) for x in xs]
        for i, (a, b) in enumerate(BLOCKS):
            part = mm_tn(xs[a], ss[b])
            if c == 0:
                total[i] = part
            else:
                total[i] += part
    riccati(lambda i: total[i], sc_ref[...], cc_ref[...], gain_ref, value_ref, work, feed)
    copies[2 * LEAF].wait()
    copies[2 * LEAF + 1].wait()
    weight = midw_ref[0]
    parent = parent_ref[0]
    core = lax.rem(lax.axis_index("col"), 2)
    w_own = jnp.where(parent == core, weight, 0.0)
    w_other = jnp.where(parent == core, 0.0, weight)

    def put(i, block):
        own_ref[i * H : (i + 1) * H, :] = (w_own * block).astype(BF16)
        other_ref[i * H : (i + 1) * H, :] = (w_other * block).astype(BF16)

    node_term(value_ref, ms, mu, put)
    tile_ref[...] = jnp.where(iota2((8, 128), 0) == parent, weight, 0.0)


def lower(count, parent, midw, leaf_s, leaf_u, mid_s, mid_u, leafw, sc, cc):
    smem = pl.BlockSpec(memory_space=pltpu.SMEM)
    vmem = pl.BlockSpec(memory_space=pltpu.VMEM)
    hbm = pl.BlockSpec(memory_space=pl.ANY)
    return pl.pallas_call(
        lower_kernel,
        out_shape=(
            jax.ShapeDtypeStruct((NU, NX), BF16),
            jax.ShapeDtypeStruct((NX, NX), BF16),
            jax.ShapeDtypeStruct((ROWS, H), BF16),
            jax.ShapeDtypeStruct((ROWS, H), BF16),
            jax.ShapeDtypeStruct((8, 128), F32),
        ),
        in_specs=[smem] * 3 + [hbm] * 4 + [vmem] * 3,
        out_specs=(vmem,) * 5,
        scratch_shapes=[
            pltpu.VMEM((LEAF * NX, NX), BF16),
            pltpu.VMEM((LEAF * NX, NU), BF16),
            pltpu.VMEM((NX, NX), BF16),
            pltpu.VMEM((NX, NU), BF16),
            pltpu.VMEM((6, H, H), F32),
            pltpu.VMEM((H, H), F32),
            pltpu.VMEM((NU, NX), F32),
            pltpu.SemaphoreType.DMA((2 * LEAF + 2,)),
        ],
        compiler_params=pltpu.CompilerParams(vmem_limit_bytes=VMEM_LIMIT),
        name="lower_nodes",
    )(count, parent, midw, leaf_s, leaf_u, mid_s, mid_u, leafw, sc, cc)


def gather_kernel(
    own_ref, other_ref, tile_ref, total_ref, tiles_ref,
    sib_buf, in_buf, out_buf, sib_send, sib_recv, send_sem, recv_sem, tile_send, tile_recv,
):
    row = lax.axis_index("row")
    col = lax.axis_index("col")
    z = col // 2
    core = lax.rem(col, 2)
    sibling = col + 1 - 2 * core
    dist = lax.rem(z + 8 - 4 * core, 8)
    is_target = dist == 0
    down = jnp.logical_and(dist >= 1, dist <= 4)
    next_z = jnp.where(down, lax.rem(z + 7, 8), lax.rem(z + 1, 8))
    next_col = 2 * next_z + core
    side = jnp.where(dist == 7, 1, 0)
    has_up = jnp.logical_and(dist != 4, dist != 5)

    barrier = pltpu.get_barrier_semaphore()

    def greet(k, carry):
        pl.semaphore_signal(
            barrier, inc=1, device_id=(row, lax.rem(col + k, 16)), device_id_type=MESH
        )
        return carry

    lax.fori_loop(1, 16, greet, 0)
    pl.semaphore_wait(barrier, 15)

    def sib_copy(c):
        rows = pl.ds(pl.multiple_of(c * CHUNK, 16), CHUNK)
        return pltpu.make_async_remote_copy(
            src_ref=other_ref.at[rows],
            dst_ref=sib_buf.at[rows],
            send_sem=sib_send.at[c],
            recv_sem=sib_recv.at[c],
            device_id=(row, sibling),
            device_id_type=MESH,
        )

    def chain_copy(c, to_side):
        rows = pl.ds(pl.multiple_of(c * CHUNK, 16), CHUNK)
        return pltpu.make_async_remote_copy(
            src_ref=out_buf.at[rows],
            dst_ref=in_buf.at[to_side, rows],
            send_sem=send_sem.at[c],
            recv_sem=recv_sem.at[to_side, c],
            device_id=(row, next_col),
            device_id_type=MESH,
        )

    def tile_copy(slot):
        return pltpu.make_async_remote_copy(
            src_ref=tile_ref,
            dst_ref=tiles_ref.at[col],
            send_sem=tile_send.at[slot],
            recv_sem=tile_recv.at[col],
            device_id=(row, 9 * slot),
            device_id_type=MESH,
        )

    def tile_arrival(source):
        return pltpu.make_async_remote_copy(
            src_ref=tile_ref,
            dst_ref=tiles_ref.at[source],
            send_sem=tile_send.at[0],
            recv_sem=tile_recv.at[source],
            device_id=(row, sibling),
            device_id_type=MESH,
        )

    def start_sib(c, carry):
        sib_copy(c).start()
        return carry

    lax.fori_loop(0, N_CHUNK, start_sib, 0)
    for slot in range(2):

        @pl.when(col != 9 * slot)
        def _():
            tile_copy(slot).start()

    def step(c, carry):
        rows = pl.ds(pl.multiple_of(c * CHUNK, 16), CHUNK)
        sib_copy(c).wait_recv()
        part = own_ref[rows, :].astype(F32) + sib_buf[rows, :].astype(F32)

        @pl.when(jnp.logical_not(has_up))
        def _():
            out_buf[rows, :] = part.astype(BF16)
            chain_copy(c, side).start()

        @pl.when(has_up)
        def _():
            chain_copy(c, 0).wait_recv()
            more = part + in_buf[0, rows, :].astype(F32)

            @pl.when(is_target)
            def _():
                chain_copy(c, 1).wait_recv()
                total_ref[rows, :] = more + in_buf[1, rows, :].astype(F32)

            @pl.when(jnp.logical_not(is_target))
            def _():
                out_buf[rows, :] = more.astype(BF16)
                chain_copy(c, side).start()

        return carry

    lax.fori_loop(0, N_CHUNK, step, 0)

    def drain(c, carry):
        sib_copy(c).wait_send()

        @pl.when(jnp.logical_not(is_target))
        def _():
            chain_copy(c, side).wait_send()

        return carry

    lax.fori_loop(0, N_CHUNK, drain, 0)
    for slot in range(2):

        @pl.when(col != 9 * slot)
        def _():
            tile_copy(slot).wait_send()

    @pl.when(is_target)
    def _():
        def arrive(k, carry):
            tile_arrival(lax.rem(col + k, 16)).wait_recv()
            return carry

        lax.fori_loop(1, 16, arrive, 0)
        tiles_ref[pl.ds(col, 1)] = tile_ref[...][None]


def gather(own, other, tile):
    vmem = pl.BlockSpec(memory_space=pltpu.VMEM)
    return pl.pallas_call(
        gather_kernel,
        out_shape=(
            jax.ShapeDtypeStruct((ROWS, H), F32),
            jax.ShapeDtypeStruct((16, 8, 128), F32),
        ),
        in_specs=[vmem] * 3,
        out_specs=(vmem,) * 2,
        scratch_shapes=[
            pltpu.VMEM((ROWS, H), BF16),
            pltpu.VMEM((2, ROWS, H), BF16),
            pltpu.VMEM((ROWS, H), BF16),
            pltpu.SemaphoreType.DMA((N_CHUNK,)),
            pltpu.SemaphoreType.DMA((N_CHUNK,)),
            pltpu.SemaphoreType.DMA((N_CHUNK,)),
            pltpu.SemaphoreType.DMA((2, N_CHUNK)),
            pltpu.SemaphoreType.DMA((2,)),
            pltpu.SemaphoreType.DMA((16,)),
        ],
        compiler_params=pltpu.CompilerParams(
            collective_id=0, has_side_effects=True, vmem_limit_bytes=VMEM_LIMIT
        ),
        name="group_sum",
    )(own, other, tile)


def upper_kernel(
    upw_ref, total_ref, tiles_ref, up_s, up_u, sc_ref, cc_ref,
    gv_ref, term_ref, wtile_ref,
    us, uu, blocks, work, feed, sems,
):
    col = lax.axis_index("col")
    core = lax.rem(col, 2)
    wtile_ref[...] = jnp.full((8, 128), upw_ref[0] + upw_ref[1], F32)

    @pl.when(col == 9 * core)
    def _():
        copies = [
            pltpu.make_async_copy(up_s.at[core], us, sems.at[0]),
            pltpu.make_async_copy(up_u.at[core], uu, sems.at[1]),
        ]
        for copy in copies:
            copy.start()
        sums = jnp.sum(tiles_ref[...], axis=0)
        weight = jnp.sum(jnp.where(iota2((8, 128), 0) == core, sums, 0.0), axis=0, keepdims=True)
        scale = 1.0 / weight[:, :1]
        for i in range(6):
            blocks[i] = total_ref[i * H : (i + 1) * H, :] * scale
        gain_ref = gv_ref.at[pl.ds(0, NU)]
        value_ref = gv_ref.at[pl.ds(NU, NX)]
        riccati(lambda i: blocks[i], sc_ref[...], cc_ref[...], gain_ref, value_ref, work, feed)
        for copy in copies:
            copy.wait()
        up_weight = upw_ref[core]

        def put(i, block):
            term_ref[i * H : (i + 1) * H, :] = (up_weight * block).astype(BF16)

        node_term(value_ref, us, uu, put)


def upper(upw, total, tiles, up_s, up_u, sc, cc):
    smem = pl.BlockSpec(memory_space=pltpu.SMEM)
    vmem = pl.BlockSpec(memory_space=pltpu.VMEM)
    hbm = pl.BlockSpec(memory_space=pl.ANY)
    return pl.pallas_call(
        upper_kernel,
        out_shape=(
            jax.ShapeDtypeStruct((GV_ROWS, NX), BF16),
            jax.ShapeDtypeStruct((ROWS, H), BF16),
            jax.ShapeDtypeStruct((8, 128), F32),
        ),
        in_specs=[smem, vmem, vmem, hbm, hbm, vmem, vmem],
        out_specs=(vmem,) * 3,
        scratch_shapes=[
            pltpu.VMEM((NX, NX), BF16),
            pltpu.VMEM((NX, NU), BF16),
            pltpu.VMEM((6, H, H), F32),
            pltpu.VMEM((H, H), F32),
            pltpu.VMEM((NU, NX), F32),
            pltpu.SemaphoreType.DMA((2,)),
        ],
        compiler_params=pltpu.CompilerParams(vmem_limit_bytes=VMEM_LIMIT),
        name="upper_nodes",
    )(upw, total, tiles, up_s, up_u, sc, cc)


def root_kernel(
    gv_ref, term_ref, wtile_ref, gvs_ref, total_ref, wtiles_ref,
    in_buf, piece_buf, pair_buf,
    w_send, w_recv, a_send, a_recv, b_send, b_recv, c_send, c_recv, s_send, s_recv,
    g_send, g_recv, gs_send, gs_recv,
):
    row = lax.axis_index("row")
    col = lax.axis_index("col")
    z = col // 2
    core = lax.rem(col, 2)
    sibling = col + 1 - 2 * core
    dist = lax.rem(z + 8 - 4 * core, 8)
    is_target = dist == 0
    barrier = pltpu.get_barrier_semaphore()

    def greet(k, carry):
        pl.semaphore_signal(
            barrier, inc=1, device_id=(row, lax.rem(col + k, 16)), device_id_type=MESH
        )
        pl.semaphore_signal(
            barrier, inc=1, device_id=(lax.rem(row + k, 16), col), device_id_type=MESH
        )
        return carry

    lax.fori_loop(1, 16, greet, 0)
    pl.semaphore_wait(barrier, 30)

    def a_copy(to_row, at):
        return pltpu.make_async_remote_copy(
            src_ref=term_ref.at[pl.ds(pl.multiple_of(to_row * PIECE, 16), PIECE)],
            dst_ref=in_buf.at[at],
            send_sem=a_send.at[to_row],
            recv_sem=a_recv.at[at],
            device_id=(to_row, col),
            device_id_type=MESH,
        )

    def b_copy(to_col, slot):
        half = lax.rem(to_col, 2)
        return pltpu.make_async_remote_copy(
            src_ref=piece_buf.at[half],
            dst_ref=pair_buf.at[slot],
            send_sem=b_send.at[to_col],
            recv_sem=b_recv.at[slot],
            device_id=(row, to_col),
            device_id_type=MESH,
        )

    def c_copy(to_row, at):
        return pltpu.make_async_remote_copy(
            src_ref=total_ref.at[at, core],
            dst_ref=total_ref.at[at, core],
            send_sem=c_send.at[to_row],
            recv_sem=c_recv.at[at],
            device_id=(to_row, col),
            device_id_type=MESH,
        )

    def s_copy(at, half):
        return pltpu.make_async_remote_copy(
            src_ref=total_ref.at[at, half],
            dst_ref=total_ref.at[at, half],
            send_sem=s_send.at[at],
            recv_sem=s_recv.at[at],
            device_id=(row, sibling),
            device_id_type=MESH,
        )

    def w_copy(to_row, at):
        return pltpu.make_async_remote_copy(
            src_ref=wtile_ref,
            dst_ref=wtiles_ref.at[at],
            send_sem=w_send.at[to_row],
            recv_sem=w_recv.at[at],
            device_id=(to_row, col),
            device_id_type=MESH,
        )

    def g_rows(c):
        return pl.ds(pl.multiple_of(c * GV_CHUNK, 16), GV_CHUNK)

    def g_copy(c, slot, to_col, lane_id):
        return pltpu.make_async_remote_copy(
            src_ref=gvs_ref.at[slot, g_rows(c)],
            dst_ref=gvs_ref.at[slot, g_rows(c)],
            send_sem=g_send.at[lane_id, c],
            recv_sem=g_recv.at[c],
            device_id=(row, to_col),
            device_id_type=MESH,
        )

    def gs_copy(c, slot):
        return pltpu.make_async_remote_copy(
            src_ref=gvs_ref.at[slot, g_rows(c)],
            dst_ref=gvs_ref.at[slot, g_rows(c)],
            send_sem=gs_send.at[c],
            recv_sem=gs_recv.at[c],
            device_id=(row, sibling),
            device_id_type=MESH,
        )

    def peers(body):
        def one(k, carry):
            body(lax.rem(row + k, 16))
            return carry

        lax.fori_loop(1, 16, one, 0)

    def columns(body):
        def one(k, carry):
            body(lax.rem(col + k, 16))
            return carry

        lax.fori_loop(1, 16, one, 0)

    def gv_chunks(body):
        def one(c, carry):
            body(c)
            return carry

        lax.fori_loop(0, N_GV, one, 0)

    up_col = 2 * lax.rem(z + 1, 8) + core
    down_col = 2 * lax.rem(z + 7, 8) + core
    to_up = dist <= 3
    to_down = jnp.logical_or(dist == 0, dist >= 6)

    def forward(c):
        @pl.when(to_up)
        def _():
            g_copy(c, core, up_col, 0).start()

        @pl.when(to_down)
        def _():
            g_copy(c, core, down_col, 1).start()

        gs_copy(c, core).start()

    peers(lambda p: w_copy(p, row).start())

    @pl.when(is_target)
    def _():
        peers(lambda p: a_copy(p, row).start())
        gvs_ref[pl.ds(core, 1)] = gv_ref[...][None]
        gv_chunks(forward)
        acc = term_ref[pl.ds(pl.multiple_of(row * PIECE, 16), PIECE), :].astype(F32)

        def add(k, acc):
            source = lax.rem(row + k, 16)
            a_copy(source, source).wait_recv()
            return acc + in_buf[source].astype(F32)

        acc = lax.fori_loop(1, 16, add, acc)
        piece = acc.astype(BF16)
        piece_buf[0] = piece[:HALF]
        piece_buf[1] = piece[HALF:]
        columns(lambda p: b_copy(p, core).start())
        pair_buf[pl.ds(core, 1)] = piece_buf[pl.ds(core, 1)]
        b_copy(col, 1 - core).wait_recv()

    @pl.when(jnp.logical_not(is_target))
    def _():
        b_copy(col, 0).wait_recv()
        b_copy(col, 1).wait_recv()

    pair = pair_buf[0].astype(F32) + pair_buf[1].astype(F32)
    total_ref[pl.ds(row, 1), pl.ds(core, 1)] = pair.astype(BF16)[None, None]
    peers(lambda p: c_copy(p, row).start())
    s_copy(row, core).start()

    @pl.when(jnp.logical_not(is_target))
    def _():
        def relay(c):
            g_copy(c, core, up_col, 0).wait_recv()
            forward(c)

        gv_chunks(relay)

    def relay_piece(p):
        c_copy(p, p).wait_recv()
        s_copy(p, core).start()

    peers(relay_piece)

    def finish(at, carry):
        s_copy(at, 1 - core).wait_recv()
        s_copy(at, core).wait_send()
        return carry

    lax.fori_loop(0, 16, finish, 0)

    def finish_peer(p):
        c_copy(p, row).wait_send()
        w_copy(p, row).wait_send()
        w_copy(p, p).wait_recv()

    peers(finish_peer)
    wtiles_ref[pl.ds(row, 1)] = wtile_ref[...][None]

    @pl.when(is_target)
    def _():
        peers(lambda p: a_copy(p, row).wait_send())
        columns(lambda p: b_copy(p, core).wait_send())

    def finish_gv(c):
        gs_copy(c, 1 - core).wait_recv()
        gs_copy(c, core).wait_send()

        @pl.when(to_up)
        def _():
            g_copy(c, core, up_col, 0).wait_send()

        @pl.when(to_down)
        def _():
            g_copy(c, core, down_col, 1).wait_send()

    gv_chunks(finish_gv)


def root_sum(gv, term, wtile):
    vmem = pl.BlockSpec(memory_space=pltpu.VMEM)
    dma = pltpu.SemaphoreType.DMA
    return pl.pallas_call(
        root_kernel,
        out_shape=(
            jax.ShapeDtypeStruct((2, GV_ROWS, NX), BF16),
            jax.ShapeDtypeStruct((16, 2, HALF, H), BF16),
            jax.ShapeDtypeStruct((16, 8, 128), F32),
        ),
        in_specs=[vmem] * 3,
        out_specs=(vmem,) * 3,
        scratch_shapes=[
            pltpu.VMEM((16, PIECE, H), BF16),
            pltpu.VMEM((2, HALF, H), BF16),
            pltpu.VMEM((2, HALF, H), BF16),
            dma((16,)), dma((16,)),
            dma((16,)), dma((16,)),
            dma((16,)), dma((2,)),
            dma((16,)), dma((16,)),
            dma((16,)), dma((16,)),
            dma((2, N_GV)), dma((N_GV,)),
            dma((N_GV,)), dma((N_GV,)),
        ],
        compiler_params=pltpu.CompilerParams(
            collective_id=1, has_side_effects=True, vmem_limit_bytes=VMEM_LIMIT
        ),
        name="root_sum",
    )(gv, term, wtile)


def down_kernel(
    count_ref, parent_ref, gvs_ref, total_ref, wtiles_ref, mid_gain_ref, root_cov_ref,
    up_s, up_u, mid_s, mid_u, leaf_s, leaf_u, sc_ref, cc_ref, nc_ref,
    root_gain_ref, root_value_ref, up_gain_out, up_value_out, up_cov_ref, mid_cov_ref, leaf_cov_out,
    us, uu, ms, mu, ls, lu, lcov, blocks, work, feed, sems, out_sems,
):
    copies = [
        pltpu.make_async_copy(up_s, us, sems.at[0]),
        pltpu.make_async_copy(up_u, uu, sems.at[1]),
        pltpu.make_async_copy(mid_s.at[0], ms, sems.at[2]),
        pltpu.make_async_copy(mid_u.at[0], mu, sems.at[3]),
        pltpu.make_async_copy(leaf_s, ls, sems.at[4]),
        pltpu.make_async_copy(leaf_u, lu, sems.at[5]),
    ]
    for copy in copies:
        copy.start()
    outs = []
    for s in range(2):
        outs.append(
            pltpu.make_async_copy(gvs_ref.at[s, pl.ds(0, NU)], up_gain_out.at[s], out_sems.at[2 * s])
        )
        outs.append(
            pltpu.make_async_copy(gvs_ref.at[s, pl.ds(NU, NX)], up_value_out.at[s], out_sems.at[2 * s + 1])
        )
    for copy in outs:
        copy.start()
    weight = jnp.sum(wtiles_ref[...], axis=0)
    scale = 1.0 / weight[:1, :1]
    for i in range(6):
        blocks[i] = total_ref[i * H : (i + 1) * H, :].astype(F32) * scale
    riccati(
        lambda i: blocks[i], sc_ref[...], cc_ref[...], root_gain_ref, root_value_ref, work, feed
    )
    noise = nc_ref[...]
    copies[0].wait()
    copies[1].wait()
    root_gain = root_gain_ref[...]
    root_cov = root_cov_ref[...]
    for s in range(2):
        store_cov(up_cov_ref.at[s], propagate(root_cov, root_gain, us[s], uu[s], noise))
    copies[2].wait()
    copies[3].wait()
    parent = parent_ref[0]
    store_cov(
        mid_cov_ref,
        propagate(up_cov_ref[parent], gvs_ref[parent, :NU, :], ms[...], mu[...], noise),
    )
    copies[4].wait()
    copies[5].wait()
    live = count_ref[0]
    mid_cov = mid_cov_ref[...]
    mid_gain = mid_gain_ref[...]
    for c in range(LEAF):
        keep = c < live
        result = propagate(mid_cov, mid_gain, ls[c], lu[c], noise)
        store_cov(lcov.at[c], [jnp.where(keep, block, jnp.zeros_like(block)) for block in result])
        out = pltpu.make_async_copy(lcov.at[c], leaf_cov_out.at[c], out_sems.at[4 + c])
        out.start()
        outs.append(out)
    for out in outs:
        out.wait()


def down(count, parent, gvs, total, wtiles, mid_gain, root_cov, up_s, up_u, mid_s, mid_u, leaf_s, leaf_u, sc, cc, nc):
    smem = pl.BlockSpec(memory_space=pltpu.SMEM)
    vmem = pl.BlockSpec(memory_space=pltpu.VMEM)
    hbm = pl.BlockSpec(memory_space=pl.ANY)
    return pl.pallas_call(
        down_kernel,
        out_shape=(
            jax.ShapeDtypeStruct((NU, NX), BF16),
            jax.ShapeDtypeStruct((NX, NX), BF16),
            jax.ShapeDtypeStruct((2, NU, NX), BF16),
            jax.ShapeDtypeStruct((2, NX, NX), BF16),
            jax.ShapeDtypeStruct((2, NX, NX), BF16),
            jax.ShapeDtypeStruct((NX, NX), BF16),
            jax.ShapeDtypeStruct((LEAF, NX, NX), BF16),
        ),
        in_specs=[smem, smem] + [vmem] * 5 + [hbm] * 6 + [vmem] * 3,
        out_specs=(vmem, vmem, hbm, hbm, vmem, vmem, hbm),
        scratch_shapes=[
            pltpu.VMEM((2, NX, NX), BF16),
            pltpu.VMEM((2, NX, NU), BF16),
            pltpu.VMEM((NX, NX), BF16),
            pltpu.VMEM((NX, NU), BF16),
            pltpu.VMEM((LEAF, NX, NX), BF16),
            pltpu.VMEM((LEAF, NX, NU), BF16),
            pltpu.VMEM((LEAF, NX, NX), BF16),
            pltpu.VMEM((6, H, H), F32),
            pltpu.VMEM((H, H), F32),
            pltpu.VMEM((NU, NX), F32),
            pltpu.SemaphoreType.DMA((6,)),
            pltpu.SemaphoreType.DMA((8,)),
        ],
        compiler_params=pltpu.CompilerParams(vmem_limit_bytes=VMEM_LIMIT),
        name="down_sweep",
    )(count, parent, gvs, total, wtiles, mid_gain, root_cov, up_s, up_u, mid_s, mid_u, leaf_s, leaf_u, sc, cc, nc)


def local(
    leaf_state_map,
    leaf_input_map,
    leaf_weight,
    leaf_count,
    mid_state_map,
    mid_input_map,
    mid_weight,
    mid_parent,
    up_state_map,
    up_input_map,
    up_weight,
    root_cov,
    state_cost,
    control_cost,
    noise_cov,
):
    sc = state_cost.reshape(1, NX)
    cc = control_cost.reshape(1, NU)
    nc = noise_cov.reshape(1, NX)
    mid_gain, mid_value, own, other, tile = lower(
        leaf_count, mid_parent, mid_weight, leaf_state_map, leaf_input_map,
        mid_state_map, mid_input_map, leaf_weight.reshape(1, LEAF), sc, cc,
    )
    total, tiles = gather(own, other, tile)
    gv, term, wtile = upper(up_weight, total, tiles, up_state_map, up_input_map, sc, cc)
    gvs, root_total, wtiles = root_sum(gv, term, wtile)
    root_gain, root_value, up_gain, up_value, up_cov, mid_cov, leaf_cov = down(
        leaf_count, mid_parent, gvs, root_total.reshape(ROWS, H), wtiles, mid_gain, root_cov,
        up_state_map, up_input_map, mid_state_map, mid_input_map, leaf_state_map, leaf_input_map,
        sc, cc, nc,
    )
    return (
        root_gain,
        root_value,
        up_gain,
        up_value,
        up_cov,
        mid_gain[None],
        mid_value[None],
        mid_cov[None],
        leaf_cov,
    )


def solution(mesh):
    both = P(("row", "col"))
    return jax.shard_map(
        local,
        mesh=mesh,
        in_specs=(
            both, both, both, both, both, both, both, both,
            P("row"), P("row"), P("row"), P(), P(), P(), P(),
        ),
        out_specs=(P(), P(), P("row"), P("row"), P("row"), both, both, both, both),
        check_vma=False,
    )
```

time: 664 us -> 112 us (0.17)
  the two profiles are of different devices: /device:TPU:26 before, /device:TPU:1 now
where the time goes in v1:
time: 112 us
  Pallas kernels  109 us (97%)
  between operations  2.77 us (2%)
    pallas_call x1, Pallas kernels, root_sum(): pl.pallas_call(root_kernel, out_shape=(jax.ShapeDtypeStruct((2, GV_ROWS,...  59 us
    pallas_call x1, Pallas kernels, gather(): pl.pallas_call(gather_kernel, out_shape=(jax.ShapeDtypeStruct((ROWS, H),...  21.5 us
    pallas_call x1, Pallas kernels, down(): pl.pallas_call(down_kernel, out_shape=(jax.ShapeDtypeStruct((NU, NX), BF1...  14.2 us
    pallas_call x1, Pallas kernels, lower(): pl.pallas_call(lower_kernel, out_shape=(jax.ShapeDtypeStruct((NU, NX), BF...  11.7 us
    pallas_call x1, Pallas kernels, upper(): pl.pallas_call(upper_kernel, out_shape=(jax.ShapeDtypeStruct((GV_ROWS, NX...  2.64 us

profile of v1, /device:TPU:1, one launch (start us, length us, event | category | flops | bytes accessed | tf_op | source)
XLA Modules:
  0.0 111.8 jit_solution(8208876094779687829)
XLA Ops:
  2.6 11.7 %lower_nodes.1 = (bf16[256,512]{1,0:T(8,128)(2,1)}, bf16[512,512]{1,0:T(8,128)(2,1)}, bf16[1536,256]{1,0:T(8,128)(2,1)}, bf16[1536,256]{1,0:T(8,128)(2,1)}, f32[8,128]{1,0:T(8,128)}) custom-call(s32[1]{0:T(128)S(6)} %copy.24.count_ref, s32[1]{0:T(128)S(6)} %copy.26.parent_ref, f32[1]{0:T(128)S(6)} %copy.25.midw_ref, bf16[4,512,512]{2,1,0:T(8,128)(2,1)} %leaf_s.3, ...), custom_call_target="tpu_custom_call" | custom-call | tf_op jit(solution)/shard_map/lower_nodes/pallas_call | solution.py:245
  14.3 21.5 %group_sum.1 = (f32[1536,256]{1,0:T(8,128)}, f32[16,8,128]{2,1,0:T(8,128)}) custom-call(bf16[1536,256]{1,0:T(8,128)(2,1)} %get-tuple-element.29.own_ref, bf16[1536,256]{1,0:T(8,128)(2,1)} %get-tuple-element.30.other_ref, f32[8,128]{1,0:T(8,128)} %get-tuple-element.31.tile_ref), custom_call_target="tpu_custom_call" | custom-call | tf_op jit(solution)/shard_map/group_sum/pallas_call | solution.py:409
  35.8 2.6 %upper_nodes.1 = (bf16[768,512]{1,0:T(8,128)(2,1)}, bf16[1536,256]{1,0:T(8,128)(2,1)}, f32[8,128]{1,0:T(8,128)}) custom-call(f32[2]{0:T(128)} %upw_ref.1, f32[1536,256]{1,0:T(8,128)} %get-tuple-element.32.total_ref, f32[16,8,128]{2,1,0:T(8,128)} %get-tuple-element.33.tiles_ref, bf16[2,512,512]{2,1,0:T(8,128)(2,1)} %up_s.3, bf16[2,512,256]{2,1,0:T(8,128)(2,1)} %up_u.3, ...), custom_call_target="tpu_custom_call" | custom-call | tf_op jit(solution)/shard_map/upper_nodes/pallas_call | solution.py:474
  38.4 59.0 %root_sum.1 = (bf16[2,768,512]{2,1,0:T(8,128)(2,1)}, bf16[16,2,48,256]{3,2,1,0:T(8,128)(2,1)}, f32[16,8,128]{2,1,0:T(8,128)}) custom-call(bf16[768,512]{1,0:T(8,128)(2,1)} %get-tuple-element.34.gv_ref, bf16[1536,256]{1,0:T(8,128)(2,1)} %get-tuple-element.35.term_ref, f32[8,128]{1,0:T(8,128)} %get-tuple-element.36.wtile_ref), custom_call_target="tpu_custom_call" | custom-call | tf_op jit(solution)/shard_map/root_sum/pallas_call | solution.py:718
  97.5 14.2 %down_sweep.1 = (bf16[256,512]{1,0:T(8,128)(2,1)}, bf16[512,512]{1,0:T(8,128)(2,1)}, bf16[2,256,512]{2,1,0:T(8,128)(2,1)}, bf16[2,512,512]{2,1,0:T(8,128)(2,1)},...) custom-call(s32[1]{0:T(128)S(6)} %copy.24.count_ref, s32[1]{0:T(128)S(6)} %copy.26.parent_ref, ...), custom_call_target="tpu_custom_call" | custom-call | tf_op jit(solution)/shard_map/down_sweep/pallas_call | solution.py:813

commit v2 on v1

--- a/solution.py
+++ b/solution.py
@@ -16,15 +16,17 @@
 F32 = jnp.float32
 BF16 = jnp.bfloat16
 MESH = pl.DeviceIdType.MESH
-VMEM_LIMIT = 56 * 1024 * 1024
-N_CHUNK = 16
+VMEM_LIMIT = 24 * 1024 * 1024
+N_CHUNK = 24
 CHUNK = ROWS // N_CHUNK
 N_GV = 12
 GV_ROWS = NX + NU
 GV_CHUNK = GV_ROWS // N_GV
 PIECE = ROWS // 16
 HALF = PIECE // 2
-REFINE_TOL = 1e-6
+ERROR_TOL = 1e-4
+MAX_CONTRACTION = 0.25
+MAX_RATIO = 256.0
 MAX_REFINE = 8
 
 
@@ -88,32 +90,39 @@
     work[...] = jnp.where(eye, 4.0 * mid / den, 0.0) - (2.0 / den) * hess
 
     def newton(_, carry):
-        x = work[...]
-        x_hi = x.astype(BF16)
+        x_hi = work[...].astype(BF16)
         res = jnp.where(eye, 1.0, 0.0) - mm(h_hi, x_hi)
-        work[...] = x + mm(x_hi, res.astype(BF16))
+        work[...] = x_hi.astype(F32) + mm(x_hi, res.astype(BF16))
         return carry
 
     lax.fori_loop(0, steps, newton, 0)
-    inv = work[...].astype(BF16)
-    feed[...] = -mm(inv, ba_hi)
+    x_hi = work[...].astype(BF16)
+    res = (jnp.where(eye, 1.0, 0.0) - mm(h_hi, x_hi)) - mm(h_lo, x_hi)
+    inv, inv_lo = split(x_hi.astype(F32) + mm(x_hi, res.astype(BF16)))
+    feed[...] = -(mm(inv, ba_hi) + (mm(inv, ba_lo) + mm(inv_lo, ba_hi)))
 
     def unconverged(state):
-        count, done = state
+        count, done, _ = state
         return jnp.logical_and(count < MAX_REFINE, done == 0)
 
     def refine(state):
-        count, _ = state
+        count, _, last = state
         f = feed[...]
         f_hi, f_lo = split(f)
         res = ba + (mm(h_hi, f_hi) + (mm(h_hi, f_lo) + mm(h_lo, f_hi)))
         step = mm(inv, res.astype(BF16))
         new = f - step
         feed[...] = new
-        small = jnp.sum(step * step) <= REFINE_TOL * jnp.sum(new * new)
-        return count + 1, small.astype(jnp.int32)
-
-    _, done = lax.while_loop(unconverged, refine, (jnp.int32(0), jnp.int32(0)))
+        size = jnp.sum(step * step)
+        norm = jnp.sum(new * new)
+        last = jnp.where(count == 0, norm, last)
+        small = jnp.logical_and(
+            size <= MAX_CONTRACTION**2 * last, size * size <= ERROR_TOL**2 * norm * last
+        )
+        return count + 1, small.astype(jnp.int32), size
+
+    first = (upper > MAX_RATIO * lower).astype(jnp.int32) * MAX_REFINE
+    _, done, _ = lax.while_loop(unconverged, refine, (first, jnp.int32(0), jnp.float32(0.0)))
 
     @pl.when(done == 0)
     def _():
@@ -191,18 +200,22 @@
 
 
 def lower_kernel(
-    count_ref, parent_ref, midw_ref, leaf_s, leaf_u, mid_s, mid_u, leafw_ref, sc_ref, cc_ref,
-    gain_ref, value_ref, own_ref, other_ref, tile_ref,
-    ls, lu, ms, mu, total, work, feed, sems,
+    count_ref, leaf_s, leaf_u, leafw_in, sc_in, cc_in,
+    gain_ref, value_ref,
+    ls, lu, leafw_ref, sc_ref, cc_ref, total, work, feed, sems,
 ):
     copies = []
+    small = []
+    for i, (src, dst) in enumerate(((leafw_in, leafw_ref), (sc_in, sc_ref), (cc_in, cc_ref))):
+        small.append(pltpu.make_async_copy(src, dst, sems.at[2 * LEAF + i]))
+        small[-1].start()
     for c in range(LEAF):
         copies.append(pltpu.make_async_copy(leaf_s.at[c], ls.at[pl.ds(c * NX, NX)], sems.at[2 * c]))
         copies.append(pltpu.make_async_copy(leaf_u.at[c], lu.at[pl.ds(c * NX, NX)], sems.at[2 * c + 1]))
-    copies.append(pltpu.make_async_copy(mid_s.at[0], ms, sems.at[2 * LEAF]))
-    copies.append(pltpu.make_async_copy(mid_u.at[0], mu, sems.at[2 * LEAF + 1]))
     for copy in copies:
         copy.start()
+    for copy in small:
+        copy.wait()
     live = count_ref[0]
     weights = leafw_ref[...].astype(F32)
     weights = jnp.where(iota2(weights.shape, 1) < live, weights, 0.0)
@@ -222,55 +235,47 @@
             else:
                 total[i] += part
     riccati(lambda i: total[i], sc_ref[...], cc_ref[...], gain_ref, value_ref, work, feed)
-    copies[2 * LEAF].wait()
-    copies[2 * LEAF + 1].wait()
-    weight = midw_ref[0]
-    parent = parent_ref[0]
-    core = lax.rem(lax.axis_index("col"), 2)
-    w_own = jnp.where(parent == core, weight, 0.0)
-    w_other = jnp.where(parent == core, 0.0, weight)
-
-    def put(i, block):
-        own_ref[i * H : (i + 1) * H, :] = (w_own * block).astype(BF16)
-        other_ref[i * H : (i + 1) * H, :] = (w_other * block).astype(BF16)
-
-    node_term(value_ref, ms, mu, put)
-    tile_ref[...] = jnp.where(iota2((8, 128), 0) == parent, weight, 0.0)
-
-
-def lower(count, parent, midw, leaf_s, leaf_u, mid_s, mid_u, leafw, sc, cc):
+
+
+def lower(count, leaf_s, leaf_u, leafw, sc, cc):
     smem = pl.BlockSpec(memory_space=pltpu.SMEM)
     vmem = pl.BlockSpec(memory_space=pltpu.VMEM)
-    hbm = pl.BlockSpec(memory_space=pl.ANY)
+    hbm = pl.BlockSpec(memory_space=pltpu.HBM)
+    leaf_s, leaf_u, leafw, sc, cc = [
+        pltpu.with_memory_space_constraint(a, pltpu.HBM) for a in (leaf_s, leaf_u, leafw, sc, cc)
+    ]
     return pl.pallas_call(
         lower_kernel,
         out_shape=(
             jax.ShapeDtypeStruct((NU, NX), BF16),
             jax.ShapeDtypeStruct((NX, NX), BF16),
-            jax.ShapeDtypeStruct((ROWS, H), BF16),
-            jax.ShapeDtypeStruct((ROWS, H), BF16),
-            jax.ShapeDtypeStruct((8, 128), F32),
         ),
-        in_specs=[smem] * 3 + [hbm] * 4 + [vmem] * 3,
-        out_specs=(vmem,) * 5,
+        in_specs=[smem] + [hbm] * 5,
+        out_specs=(vmem,) * 2,
         scratch_shapes=[
             pltpu.VMEM((LEAF * NX, NX), BF16),
             pltpu.VMEM((LEAF * NX, NU), BF16),
-            pltpu.VMEM((NX, NX), BF16),
-            pltpu.VMEM((NX, NU), BF16),
+            pltpu.VMEM((1, LEAF), BF16),
+            pltpu.VMEM((1, NX), F32),
+            pltpu.VMEM((1, NU), F32),
             pltpu.VMEM((6, H, H), F32),
             pltpu.VMEM((H, H), F32),
             pltpu.VMEM((NU, NX), F32),
-            pltpu.SemaphoreType.DMA((2 * LEAF + 2,)),
+            pltpu.SemaphoreType.DMA((2 * LEAF + 3,)),
         ],
         compiler_params=pltpu.CompilerParams(vmem_limit_bytes=VMEM_LIMIT),
+        cost_estimate=pl.CostEstimate(
+            flops=LEAF * NX * 2 * (NX + NU) ** 2, bytes_accessed=LEAF * NX * (NX + NU) * 2, transcendentals=0
+        ),
         name="lower_nodes",
-    )(count, parent, midw, leaf_s, leaf_u, mid_s, mid_u, leafw, sc, cc)
+    )(count, leaf_s, leaf_u, leafw, sc, cc)
 
 
 def gather_kernel(
-    own_ref, other_ref, tile_ref, total_ref, tiles_ref,
-    sib_buf, in_buf, out_buf, sib_send, sib_recv, send_sem, recv_sem, tile_send, tile_recv,
+    parent_ref, midw_ref, value_ref, mid_s, mid_u,
+    total_ref, weight_ref,
+    own_buf, other_buf, sib_buf, in_buf, out_buf, tile, sib_tile, in_tile, out_tile,
+    sib_send, sib_recv, send_sem, recv_sem,
 ):
     row = lax.axis_index("row")
     col = lax.axis_index("col")
@@ -280,62 +285,55 @@
     dist = lax.rem(z + 8 - 4 * core, 8)
     is_target = dist == 0
     down = jnp.logical_and(dist >= 1, dist <= 4)
-    next_z = jnp.where(down, lax.rem(z + 7, 8), lax.rem(z + 1, 8))
-    next_col = 2 * next_z + core
+    up_col = 2 * lax.rem(z + 1, 8) + core
+    down_col = 2 * lax.rem(z + 7, 8) + core
+    next_col = jnp.where(down, down_col, up_col)
     side = jnp.where(dist == 7, 1, 0)
     has_up = jnp.logical_and(dist != 4, dist != 5)
 
     barrier = pltpu.get_barrier_semaphore()
-
-    def greet(k, carry):
-        pl.semaphore_signal(
-            barrier, inc=1, device_id=(row, lax.rem(col + k, 16)), device_id_type=MESH
-        )
-        return carry
-
-    lax.fori_loop(1, 16, greet, 0)
-    pl.semaphore_wait(barrier, 15)
+    for peer in (sibling, up_col, down_col):
+        pl.semaphore_signal(barrier, inc=1, device_id=(row, peer), device_id_type=MESH)
+    weight = midw_ref[0]
+    parent = parent_ref[0]
+    w_own = jnp.where(parent == core, weight, 0.0)
+    w_other = jnp.where(parent == core, 0.0, weight)
+
+    def put(i, block):
+        own_buf[i * H : (i + 1) * H, :] = w_own * block
+        other_buf[i * H : (i + 1) * H, :] = (w_other * block).astype(BF16)
+
+    node_term(value_ref, mid_s.at[0], mid_u.at[0], put)
+    tile[...] = jnp.where(iota2((8, 128), 0) == parent, weight, 0.0)
+    pl.semaphore_wait(barrier, 3)
+
+    def chunk(c):
+        return pl.ds(pl.multiple_of(c * CHUNK, 16), CHUNK)
+
+    def remote(src, dst, send, recv, peer):
+        return pltpu.make_async_remote_copy(
+            src_ref=src, dst_ref=dst, send_sem=send, recv_sem=recv,
+            device_id=(row, peer), device_id_type=MESH,
+        )
 
     def sib_copy(c):
-        rows = pl.ds(pl.multiple_of(c * CHUNK, 16), CHUNK)
-        return pltpu.make_async_remote_copy(
-            src_ref=other_ref.at[rows],
-            dst_ref=sib_buf.at[rows],
-            send_sem=sib_send.at[c],
-            recv_sem=sib_recv.at[c],
-            device_id=(row, sibling),
-            device_id_type=MESH,
+        return remote(
+            other_buf.at[chunk(c)], sib_buf.at[chunk(c)], sib_send.at[c], sib_recv.at[c], sibling
         )
 
     def chain_copy(c, to_side):
-        rows = pl.ds(pl.multiple_of(c * CHUNK, 16), CHUNK)
-        return pltpu.make_async_remote_copy(
-            src_ref=out_buf.at[rows],
-            dst_ref=in_buf.at[to_side, rows],
-            send_sem=send_sem.at[c],
-            recv_sem=recv_sem.at[to_side, c],
-            device_id=(row, next_col),
-            device_id_type=MESH,
-        )
-
-    def tile_copy(slot):
-        return pltpu.make_async_remote_copy(
-            src_ref=tile_ref,
-            dst_ref=tiles_ref.at[col],
-            send_sem=tile_send.at[slot],
-            recv_sem=tile_recv.at[col],
-            device_id=(row, 9 * slot),
-            device_id_type=MESH,
-        )
-
-    def tile_arrival(source):
-        return pltpu.make_async_remote_copy(
-            src_ref=tile_ref,
-            dst_ref=tiles_ref.at[source],
-            send_sem=tile_send.at[0],
-            recv_sem=tile_recv.at[source],
-            device_id=(row, sibling),
-            device_id_type=MESH,
+        return remote(
+            out_buf.at[chunk(c)], in_buf.at[to_side, chunk(c)],
+            send_sem.at[c], recv_sem.at[to_side, c], next_col,
+        )
+
+    def sib_tile_copy():
+        return remote(tile, sib_tile, sib_send.at[N_CHUNK], sib_recv.at[N_CHUNK], sibling)
+
+    def tile_copy(to_side):
+        return remote(
+            out_tile, in_tile.at[to_side],
+            send_sem.at[N_CHUNK], recv_sem.at[to_side, N_CHUNK], next_col,
         )
 
     def start_sib(c, carry):
@@ -343,16 +341,12 @@
         return carry
 
     lax.fori_loop(0, N_CHUNK, start_sib, 0)
-    for slot in range(2):
-
-        @pl.when(col != 9 * slot)
-        def _():
-            tile_copy(slot).start()
+    sib_tile_copy().start()
 
     def step(c, carry):
-        rows = pl.ds(pl.multiple_of(c * CHUNK, 16), CHUNK)
+        rows = chunk(c)
         sib_copy(c).wait_recv()
-        part = own_ref[rows, :].astype(F32) + sib_buf[rows, :].astype(F32)
+        part = own_buf[rows, :] + sib_buf[rows, :].astype(F32)
 
         @pl.when(jnp.logical_not(has_up))
         def _():
@@ -377,6 +371,28 @@
         return carry
 
     lax.fori_loop(0, N_CHUNK, step, 0)
+    sib_tile_copy().wait_recv()
+    tiles = tile[...] + sib_tile[...]
+
+    @pl.when(jnp.logical_not(has_up))
+    def _():
+        out_tile[...] = tiles
+        tile_copy(side).start()
+
+    @pl.when(has_up)
+    def _():
+        tile_copy(0).wait_recv()
+        more = tiles + in_tile[0]
+
+        @pl.when(is_target)
+        def _():
+            tile_copy(1).wait_recv()
+            weight_ref[...] = more + in_tile[1]
+
+        @pl.when(jnp.logical_not(is_target))
+        def _():
+            out_tile[...] = more
+            tile_copy(side).start()
 
     def drain(c, carry):
         sib_copy(c).wait_send()
@@ -388,114 +404,82 @@
         return carry
 
     lax.fori_loop(0, N_CHUNK, drain, 0)
-    for slot in range(2):
-
-        @pl.when(col != 9 * slot)
-        def _():
-            tile_copy(slot).wait_send()
-
-    @pl.when(is_target)
-    def _():
-        def arrive(k, carry):
-            tile_arrival(lax.rem(col + k, 16)).wait_recv()
-            return carry
-
-        lax.fori_loop(1, 16, arrive, 0)
-        tiles_ref[pl.ds(col, 1)] = tile_ref[...][None]
-
-
-def gather(own, other, tile):
+    sib_tile_copy().wait_send()
+
+    @pl.when(jnp.logical_not(is_target))
+    def _():
+        tile_copy(side).wait_send()
+
+
+def gather(parent, midw, value, mid_s, mid_u):
+    smem = pl.BlockSpec(memory_space=pltpu.SMEM)
     vmem = pl.BlockSpec(memory_space=pltpu.VMEM)
+    dma = pltpu.SemaphoreType.DMA
     return pl.pallas_call(
         gather_kernel,
         out_shape=(
             jax.ShapeDtypeStruct((ROWS, H), F32),
-            jax.ShapeDtypeStruct((16, 8, 128), F32),
+            jax.ShapeDtypeStruct((8, 128), F32),
         ),
-        in_specs=[vmem] * 3,
+        in_specs=[smem, smem, vmem, vmem, vmem],
         out_specs=(vmem,) * 2,
         scratch_shapes=[
+            pltpu.VMEM((ROWS, H), F32),
+            pltpu.VMEM((ROWS, H), BF16),
             pltpu.VMEM((ROWS, H), BF16),
             pltpu.VMEM((2, ROWS, H), BF16),
             pltpu.VMEM((ROWS, H), BF16),
-            pltpu.SemaphoreType.DMA((N_CHUNK,)),
-            pltpu.SemaphoreType.DMA((N_CHUNK,)),
-            pltpu.SemaphoreType.DMA((N_CHUNK,)),
-            pltpu.SemaphoreType.DMA((2, N_CHUNK)),
-            pltpu.SemaphoreType.DMA((2,)),
-            pltpu.SemaphoreType.DMA((16,)),
+            pltpu.VMEM((8, 128), F32),
+            pltpu.VMEM((8, 128), F32),
+            pltpu.VMEM((2, 8, 128), F32),
+            pltpu.VMEM((8, 128), F32),
+            dma((N_CHUNK + 1,)),
+            dma((N_CHUNK + 1,)),
+            dma((N_CHUNK + 1,)),
+            dma((2, N_CHUNK + 1)),
         ],
         compiler_params=pltpu.CompilerParams(
             collective_id=0, has_side_effects=True, vmem_limit_bytes=VMEM_LIMIT
         ),
         name="group_sum",
-    )(own, other, tile)
-
-
-def upper_kernel(
-    upw_ref, total_ref, tiles_ref, up_s, up_u, sc_ref, cc_ref,
-    gv_ref, term_ref, wtile_ref,
-    us, uu, blocks, work, feed, sems,
-):
+    )(parent, midw, value, mid_s, mid_u)
+
+
+def upper_kernel(total_ref, weight_ref, sc_ref, cc_ref, gv_ref, blocks, work, feed):
     col = lax.axis_index("col")
     core = lax.rem(col, 2)
-    wtile_ref[...] = jnp.full((8, 128), upw_ref[0] + upw_ref[1], F32)
 
     @pl.when(col == 9 * core)
     def _():
-        copies = [
-            pltpu.make_async_copy(up_s.at[core], us, sems.at[0]),
-            pltpu.make_async_copy(up_u.at[core], uu, sems.at[1]),
-        ]
-        for copy in copies:
-            copy.start()
-        sums = jnp.sum(tiles_ref[...], axis=0)
-        weight = jnp.sum(jnp.where(iota2((8, 128), 0) == core, sums, 0.0), axis=0, keepdims=True)
-        scale = 1.0 / weight[:, :1]
+        picked = jnp.where(iota2((8, 128), 0) == core, weight_ref[...], 0.0)
+        scale = 1.0 / jnp.sum(picked, axis=0, keepdims=True)[:, :1]
         for i in range(6):
             blocks[i] = total_ref[i * H : (i + 1) * H, :] * scale
         gain_ref = gv_ref.at[pl.ds(0, NU)]
         value_ref = gv_ref.at[pl.ds(NU, NX)]
         riccati(lambda i: blocks[i], sc_ref[...], cc_ref[...], gain_ref, value_ref, work, feed)
-        for copy in copies:
-            copy.wait()
-        up_weight = upw_ref[core]
-
-        def put(i, block):
-            term_ref[i * H : (i + 1) * H, :] = (up_weight * block).astype(BF16)
-
-        node_term(value_ref, us, uu, put)
-
-
-def upper(upw, total, tiles, up_s, up_u, sc, cc):
-    smem = pl.BlockSpec(memory_space=pltpu.SMEM)
+
+
+def upper(total, weight, sc, cc):
     vmem = pl.BlockSpec(memory_space=pltpu.VMEM)
-    hbm = pl.BlockSpec(memory_space=pl.ANY)
     return pl.pallas_call(
         upper_kernel,
-        out_shape=(
-            jax.ShapeDtypeStruct((GV_ROWS, NX), BF16),
-            jax.ShapeDtypeStruct((ROWS, H), BF16),
-            jax.ShapeDtypeStruct((8, 128), F32),
-        ),
-        in_specs=[smem, vmem, vmem, hbm, hbm, vmem, vmem],
-        out_specs=(vmem,) * 3,
+        out_shape=jax.ShapeDtypeStruct((GV_ROWS, NX), BF16),
+        in_specs=[vmem] * 4,
+        out_specs=vmem,
         scratch_shapes=[
-            pltpu.VMEM((NX, NX), BF16),
-            pltpu.VMEM((NX, NU), BF16),
             pltpu.VMEM((6, H, H), F32),
             pltpu.VMEM((H, H), F32),
             pltpu.VMEM((NU, NX), F32),
-            pltpu.SemaphoreType.DMA((2,)),
         ],
         compiler_params=pltpu.CompilerParams(vmem_limit_bytes=VMEM_LIMIT),
         name="upper_nodes",
-    )(upw, total, tiles, up_s, up_u, sc, cc)
+    )(total, weight, sc, cc)
 
 
 def root_kernel(
-    gv_ref, term_ref, wtile_ref, gvs_ref, total_ref, wtiles_ref,
-    in_buf, piece_buf, pair_buf,
+    upw_ref, gv_ref, up_s, up_u, gvs_ref, total_ref, wtiles_ref,
+    term_ref, wtile_ref, in_buf, piece_buf, pair_buf,
     w_send, w_recv, a_send, a_recv, b_send, b_recv, c_send, c_recv, s_send, s_recv,
     g_send, g_recv, gs_send, gs_recv,
 ):
@@ -518,6 +502,18 @@
         return carry
 
     lax.fori_loop(1, 16, greet, 0)
+    wtile_ref[...] = jnp.full((8, 128), upw_ref[0] + upw_ref[1], F32)
+
+    @pl.when(is_target)
+    def _():
+        gvs_ref[pl.ds(core, 1)] = gv_ref[...][None]
+        up_weight = jnp.where(core == 0, upw_ref[0], upw_ref[1])
+
+        def put(i, block):
+            term_ref[i * H : (i + 1) * H, :] = (up_weight * block).astype(BF16)
+
+        node_term(gv_ref.at[pl.ds(NU, NX)], up_s.at[core], up_u.at[core], put)
+
     pl.semaphore_wait(barrier, 30)
 
     def a_copy(to_row, at):
@@ -608,12 +604,12 @@
 
         lax.fori_loop(1, 16, one, 0)
 
-    def gv_chunks(body):
+    def gv_chunks(body, first=0, last=N_GV):
         def one(c, carry):
             body(c)
             return carry
 
-        lax.fori_loop(0, N_GV, one, 0)
+        lax.fori_loop(first, last, one, 0)
 
     up_col = 2 * lax.rem(z + 1, 8) + core
     down_col = 2 * lax.rem(z + 7, 8) + core
@@ -631,12 +627,14 @@
 
         gs_copy(c, core).start()
 
+    @pl.when(is_target)
+    def _():
+        peers(lambda p: a_copy(p, row).start())
+
     peers(lambda p: w_copy(p, row).start())
 
     @pl.when(is_target)
     def _():
-        peers(lambda p: a_copy(p, row).start())
-        gvs_ref[pl.ds(core, 1)] = gv_ref[...][None]
         gv_chunks(forward)
         acc = term_ref[pl.ds(pl.multiple_of(row * PIECE, 16), PIECE), :].astype(F32)
 
@@ -653,8 +651,16 @@
         pair_buf[pl.ds(core, 1)] = piece_buf[pl.ds(core, 1)]
         b_copy(col, 1 - core).wait_recv()
 
+    def relay(c):
+        g_copy(c, core, up_col, 0).wait_recv()
+        forward(c)
+
+    hops = jnp.minimum(dist, 8 - dist)
+    early = jnp.where(hops <= 2, N_GV, jnp.where(hops == 3, N_GV // 2, 0))
+
     @pl.when(jnp.logical_not(is_target))
     def _():
+        gv_chunks(relay, 0, early)
         b_copy(col, 0).wait_recv()
         b_copy(col, 1).wait_recv()
 
@@ -665,11 +671,7 @@
 
     @pl.when(jnp.logical_not(is_target))
     def _():
-        def relay(c):
-            g_copy(c, core, up_col, 0).wait_recv()
-            forward(c)
-
-        gv_chunks(relay)
+        gv_chunks(relay, early, N_GV)
 
     def relay_piece(p):
         c_copy(p, p).wait_recv()
@@ -712,7 +714,8 @@
     gv_chunks(finish_gv)
 
 
-def root_sum(gv, term, wtile):
+def root_sum(upw, gv, up_s, up_u):
+    smem = pl.BlockSpec(memory_space=pltpu.SMEM)
     vmem = pl.BlockSpec(memory_space=pltpu.VMEM)
     dma = pltpu.SemaphoreType.DMA
     return pl.pallas_call(
@@ -722,9 +725,11 @@
             jax.ShapeDtypeStruct((16, 2, HALF, H), BF16),
             jax.ShapeDtypeStruct((16, 8, 128), F32),
         ),
-        in_specs=[vmem] * 3,
+        in_specs=[smem, vmem, vmem, vmem],
         out_specs=(vmem,) * 3,
         scratch_shapes=[
+            pltpu.VMEM((ROWS, H), BF16),
+            pltpu.VMEM((8, 128), F32),
             pltpu.VMEM((16, PIECE, H), BF16),
             pltpu.VMEM((2, HALF, H), BF16),
             pltpu.VMEM((2, HALF, H), BF16),
@@ -740,35 +745,28 @@
             collective_id=1, has_side_effects=True, vmem_limit_bytes=VMEM_LIMIT
         ),
         name="root_sum",
-    )(gv, term, wtile)
+    )(upw, gv, up_s, up_u)
 
 
 def down_kernel(
-    count_ref, parent_ref, gvs_ref, total_ref, wtiles_ref, mid_gain_ref, root_cov_ref,
+    count_ref, parent_ref, gvs_ref, total_ref, wtiles_ref, mid_gain_ref, mid_value_ref, root_cov_ref,
     up_s, up_u, mid_s, mid_u, leaf_s, leaf_u, sc_ref, cc_ref, nc_ref,
-    root_gain_ref, root_value_ref, up_gain_out, up_value_out, up_cov_ref, mid_cov_ref, leaf_cov_out,
-    us, uu, ms, mu, ls, lu, lcov, blocks, work, feed, sems, out_sems,
+    root_gain_out, root_value_out, up_gain_out, up_value_out, up_cov_out,
+    mid_gain_out, mid_value_out, mid_cov_out, leaf_cov_out,
+    root_gain_ref, root_value_ref, up_cov_ref, mid_cov_ref, lcov, blocks, work, feed, out_sems,
 ):
-    copies = [
-        pltpu.make_async_copy(up_s, us, sems.at[0]),
-        pltpu.make_async_copy(up_u, uu, sems.at[1]),
-        pltpu.make_async_copy(mid_s.at[0], ms, sems.at[2]),
-        pltpu.make_async_copy(mid_u.at[0], mu, sems.at[3]),
-        pltpu.make_async_copy(leaf_s, ls, sems.at[4]),
-        pltpu.make_async_copy(leaf_u, lu, sems.at[5]),
-    ]
-    for copy in copies:
+    outs = []
+
+    def emit(src, dst):
+        copy = pltpu.make_async_copy(src, dst, out_sems.at[len(outs)])
         copy.start()
-    outs = []
+        outs.append(copy)
+
     for s in range(2):
-        outs.append(
-            pltpu.make_async_copy(gvs_ref.at[s, pl.ds(0, NU)], up_gain_out.at[s], out_sems.at[2 * s])
-        )
-        outs.append(
-            pltpu.make_async_copy(gvs_ref.at[s, pl.ds(NU, NX)], up_value_out.at[s], out_sems.at[2 * s + 1])
-        )
-    for copy in outs:
-        copy.start()
+        emit(gvs_ref.at[s, pl.ds(0, NU)], up_gain_out.at[s])
+        emit(gvs_ref.at[s, pl.ds(NU, NX)], up_value_out.at[s])
+    emit(mid_gain_ref, mid_gain_out)
+    emit(mid_value_ref, mid_value_out)
     weight = jnp.sum(wtiles_ref[...], axis=0)
     scale = 1.0 / weight[:1, :1]
     for i in range(6):
@@ -776,37 +774,33 @@
     riccati(
         lambda i: blocks[i], sc_ref[...], cc_ref[...], root_gain_ref, root_value_ref, work, feed
     )
+    emit(root_gain_ref, root_gain_out)
+    emit(root_value_ref, root_value_out)
     noise = nc_ref[...]
-    copies[0].wait()
-    copies[1].wait()
     root_gain = root_gain_ref[...]
     root_cov = root_cov_ref[...]
     for s in range(2):
-        store_cov(up_cov_ref.at[s], propagate(root_cov, root_gain, us[s], uu[s], noise))
-    copies[2].wait()
-    copies[3].wait()
+        store_cov(up_cov_ref.at[s], propagate(root_cov, root_gain, up_s[s], up_u[s], noise))
+        emit(up_cov_ref.at[s], up_cov_out.at[s])
     parent = parent_ref[0]
     store_cov(
         mid_cov_ref,
-        propagate(up_cov_ref[parent], gvs_ref[parent, :NU, :], ms[...], mu[...], noise),
+        propagate(up_cov_ref[parent], gvs_ref[parent, :NU, :], mid_s[0], mid_u[0], noise),
     )
-    copies[4].wait()
-    copies[5].wait()
+    emit(mid_cov_ref, mid_cov_out)
     live = count_ref[0]
     mid_cov = mid_cov_ref[...]
     mid_gain = mid_gain_ref[...]
     for c in range(LEAF):
         keep = c < live
-        result = propagate(mid_cov, mid_gain, ls[c], lu[c], noise)
+        result = propagate(mid_cov, mid_gain, leaf_s[c], leaf_u[c], noise)
         store_cov(lcov.at[c], [jnp.where(keep, block, jnp.zeros_like(block)) for block in result])
-        out = pltpu.make_async_copy(lcov.at[c], leaf_cov_out.at[c], out_sems.at[4 + c])
-        out.start()
-        outs.append(out)
+        emit(lcov.at[c], leaf_cov_out.at[c])
     for out in outs:
         out.wait()
 
 
-def down(count, parent, gvs, total, wtiles, mid_gain, root_cov, up_s, up_u, mid_s, mid_u, leaf_s, leaf_u, sc, cc, nc):
+def down(count, parent, *arrays):
     smem = pl.BlockSpec(memory_space=pltpu.SMEM)
     vmem = pl.BlockSpec(memory_space=pltpu.VMEM)
     hbm = pl.BlockSpec(memory_space=pl.ANY)
@@ -818,28 +812,27 @@
             jax.ShapeDtypeStruct((2, NU, NX), BF16),
             jax.ShapeDtypeStruct((2, NX, NX), BF16),
             jax.ShapeDtypeStruct((2, NX, NX), BF16),
+            jax.ShapeDtypeStruct((NU, NX), BF16),
+            jax.ShapeDtypeStruct((NX, NX), BF16),
             jax.ShapeDtypeStruct((NX, NX), BF16),
             jax.ShapeDtypeStruct((LEAF, NX, NX), BF16),
         ),
-        in_specs=[smem, smem] + [vmem] * 5 + [hbm] * 6 + [vmem] * 3,
-        out_specs=(vmem, vmem, hbm, hbm, vmem, vmem, hbm),
+        in_specs=[smem, smem] + [vmem] * len(arrays),
+        out_specs=(hbm,) * 9,
         scratch_shapes=[
+            pltpu.VMEM((NU, NX), BF16),
+            pltpu.VMEM((NX, NX), BF16),
             pltpu.VMEM((2, NX, NX), BF16),
-            pltpu.VMEM((2, NX, NU), BF16),
             pltpu.VMEM((NX, NX), BF16),
-            pltpu.VMEM((NX, NU), BF16),
-            pltpu.VMEM((LEAF, NX, NX), BF16),
-            pltpu.VMEM((LEAF, NX, NU), BF16),
             pltpu.VMEM((LEAF, NX, NX), BF16),
             pltpu.VMEM((6, H, H), F32),
             pltpu.VMEM((H, H), F32),
             pltpu.VMEM((NU, NX), F32),
-            pltpu.SemaphoreType.DMA((6,)),
-            pltpu.SemaphoreType.DMA((8,)),
+            pltpu.SemaphoreType.DMA((15,)),
         ],
         compiler_params=pltpu.CompilerParams(vmem_limit_bytes=VMEM_LIMIT),
         name="down_sweep",
-    )(count, parent, gvs, total, wtiles, mid_gain, root_cov, up_s, up_u, mid_s, mid_u, leaf_s, leaf_u, sc, cc, nc)
+    )(count, parent, *arrays)
 
 
 def local(
@@ -862,18 +855,18 @@
     sc = state_cost.reshape(1, NX)
     cc = control_cost.reshape(1, NU)
     nc = noise_cov.reshape(1, NX)
-    mid_gain, mid_value, own, other, tile = lower(
-        leaf_count, mid_parent, mid_weight, leaf_state_map, leaf_input_map,
-        mid_state_map, mid_input_map, leaf_weight.reshape(1, LEAF), sc, cc,
+    mid_gain, mid_value = lower(
+        leaf_count, leaf_state_map, leaf_input_map, leaf_weight.reshape(1, LEAF), sc, cc
     )
-    total, tiles = gather(own, other, tile)
-    gv, term, wtile = upper(up_weight, total, tiles, up_state_map, up_input_map, sc, cc)
-    gvs, root_total, wtiles = root_sum(gv, term, wtile)
-    root_gain, root_value, up_gain, up_value, up_cov, mid_cov, leaf_cov = down(
-        leaf_count, mid_parent, gvs, root_total.reshape(ROWS, H), wtiles, mid_gain, root_cov,
-        up_state_map, up_input_map, mid_state_map, mid_input_map, leaf_state_map, leaf_input_map,
-        sc, cc, nc,
+    total, weight = gather(mid_parent, mid_weight, mid_value, mid_state_map, mid_input_map)
+    gv = upper(total, weight, sc, cc)
+    gvs, root_total, wtiles = root_sum(up_weight, gv, up_state_map, up_input_map)
+    outs = down(
+        leaf_count, mid_parent, gvs, root_total.reshape(ROWS, H), wtiles, mid_gain, mid_value,
+        root_cov, up_state_map, up_input_map, mid_state_map, mid_input_map,
+        leaf_state_map, leaf_input_map, sc, cc, nc,
     )
+    root_gain, root_value, up_gain, up_value, up_cov, mid_gain, mid_value, mid_cov, leaf_cov = outs
     return (
         root_gain,
         root_value,

time: 112 us -> 86.7 us (0.77)
  Pallas kernels: 109 us -> 83.6 us
    pallas_call x1, Pallas kernels: 59 us -> 45.9 us  [root_sum(): pl.pallas_call(root_kernel, out_shape=(jax.ShapeDtypeStruct((2, GV_ROWS,...]
    pallas_call x1, Pallas kernels: 14.2 us -> 10.4 us  [down(): pl.pallas_call(down_kernel, out_shape=(jax.ShapeDtypeStruct((NU, NX), BF1...]
    pallas_call x1, Pallas kernels: 21.5 us -> 18.4 us  [gather(): pl.pallas_call(gather_kernel, out_shape=(jax.ShapeDtypeStruct((ROWS, H),...]
    pallas_call x1, Pallas kernels: 11.7 us -> 8.9 us  [lower(): pl.pallas_call(lower_kernel, out_shape=(jax.ShapeDtypeStruct((NU, NX), BF...]
    pallas_call x1, Pallas kernels: 2.64 us -> 0.02 us  [upper(): pl.pallas_call(upper_kernel, out_shape=jax.ShapeDtypeStruct((GV_ROWS, NX)...]
where the time goes in v2:
time: 86.7 us; the launch traced here: 86.6 us
  Pallas kernels  83.6 us (96%)
  between operations  2.95 us (3%)
    pallas_call x1, Pallas kernels, root_sum(): pl.pallas_call(root_kernel, out_shape=(jax.ShapeDtypeStruct((2, GV_ROWS,...  45.9 us
    pallas_call x1, Pallas kernels, gather(): pl.pallas_call(gather_kernel, out_shape=(jax.ShapeDtypeStruct((ROWS, H),...  18.4 us
    pallas_call x1, Pallas kernels, down(): pl.pallas_call(down_kernel, out_shape=(jax.ShapeDtypeStruct((NU, NX), BF1...  10.4 us
    pallas_call x1, Pallas kernels, lower(): pl.pallas_call(lower_kernel, out_shape=(jax.ShapeDtypeStruct((NU, NX), BF...  8.9 us

profile of v2, /device:TPU:1, one launch (start us, length us, event | category | flops | bytes accessed | tf_op | source)
XLA Modules:
  0.0 86.6 jit_solution(10407140054243475969)
XLA Ops:
  2.6 0.0 copy-start.2
  2.6 0.0 copy-start.5
  2.6 0.0 copy-start.7
  2.6 0.0 copy-start.8
  2.6 8.9 %lower_nodes.1 = (bf16[256,512]{1,0:T(8,128)(2,1)S(1)}, bf16[512,512]{1,0:T(8,128)(2,1)S(1)}) custom-call(s32[1]{0:T(128)S(6)} %copy.24.count_ref, bf16[4,512,512]{2,1,0:T(8,128)(2,1)} %leaf_s.3, bf16[4,512,256]{2,1,0:T(8,128)(2,1)} %leaf_u.3, bf16[1,4]{1,0:T(2,128)(2,1)} %bitcast.19, f32[1,512]{1,0:T(1,128)} %bitcast.9, f32[1,256]{1,0:T(1,128)} %bitcast.12), custom_call_target="tpu_custom_call" | custom-call | flops 2415919104 | bytes 3145728 | tf_op jit(solution)/shard_map/lower_nodes/pallas_call | solution.py:247
  11.5 0.0 copy-start
  11.5 0.0 copy-start.1
  11.6 0.0 copy-start.10
  11.6 0.0 copy-done.2
  11.6 0.0 copy-done.5
  11.6 18.4 %group_sum.1 = (f32[1536,256]{1,0:T(8,128)S(1)}, f32[8,128]{1,0:T(8,128)S(1)}) custom-call(s32[1]{0:T(128)S(6)} %copy.26.parent_ref, f32[1]{0:T(128)S(6)} %copy.25.midw_ref, bf16[512,512]{1,0:T(8,128)(2,1)S(1)} %get-tuple-element.25.value_ref.mid_value_ref, bf16[1,512,512]{2,1,0:T(8,128)(2,1)S(1)} %copy-done.2, bf16[1,512,256]{2,1,0:T(8,128)(2,1)S(1)} %copy-done.5), custom_call_target="tpu_custom_call" | custom-call | tf_op jit(solution)/shard_map/group_sum/pallas_call | solution.py:418
  29.9 0.0 copy-done.7
  30.0 0.0 copy-done.8
  30.0 0.0 copy-start.3
  30.0 0.0 copy-start.4
  30.0 0.0 copy-start.6
  30.0 0.0 copy-start.9
  30.0 0.0 copy-done
  30.0 0.0 copy-done.1
  30.1 0.0 copy-done.10
  30.1 45.9 %root_sum.1 = (bf16[2,768,512]{2,1,0:T(8,128)(2,1)S(1)}, bf16[16,2,48,256]{3,2,1,0:T(8,128)(2,1)S(1)}, f32[16,8,128]{2,1,0:T(8,128)S(1)}) custom-call(f32[2]{0:T(128)S(1)} %copy-done.10, bf16[768,512]{1,0:T(8,128)(2,1)S(1)} %upper_nodes.1.gv_ref, bf16[2,512,512]{2,1,0:T(8,128)(2,1)S(1)} %copy-done, bf16[2,512,256]{2,1,0:T(8,128)(2,1)S(1)} %copy-done.1), custom_call_target="tpu_custom_call" | custom-call | tf_op jit(solution)/shard_map/root_sum/pallas_call | solution.py:721
  76.0 0.0 copy-done.3
  76.0 0.0 copy-done.4
  76.0 0.0 copy-done.6
  76.0 0.0 copy-done.9
  76.0 10.4 %down_sweep.1 = (bf16[256,512]{1,0:T(8,128)(2,1)}, bf16[512,512]{1,0:T(8,128)(2,1)}, bf16[2,256,512]{2,1,0:T(8,128)(2,1)}, bf16[2,512,512]{2,1,0:T(8,128)(2,1)},...) custom-call(s32[1]{0:T(128)S(6)} %copy.24.count_ref, ...), custom_call_target="tpu_custom_call" | custom-call | tf_op jit(solution)/shard_map/down_sweep/pallas_call | solution.py:807
  (1 shorter events, 0.0 us)
Async XLA Ops:
  2.6 9.0 %copy-start.2 = (bf16[1,512,512]{2,1,0:T(8,128)(2,1)S(1)}, bf16[1,512,512]{2,1,0:T(8,128)(2,1)}, u32[]{:S(2)}) copy-start(bf16[1,512,512]{2,1,0:T(8,128)(2,1)} %mid_s.3) | copy-start | bytes 1572868
  2.6 9.0 %copy-start.5 = (bf16[1,512,256]{2,1,0:T(8,128)(2,1)S(1)}, bf16[1,512,256]{2,1,0:T(8,128)(2,1)}, u32[]{:S(2)}) copy-start(bf16[1,512,256]{2,1,0:T(8,128)(2,1)} %mid_u.3) | copy-start | bytes 786436
  2.6 27.3 %copy-start.7 = (f32[512]{0:T(512)S(1)}, f32[512]{0:T(512)}, u32[]{:S(2)}) copy-start(f32[512]{0:T(512)} %param.27) | copy-start | bytes 6148
  2.6 27.3 %copy-start.8 = (f32[256]{0:T(256)S(1)}, f32[256]{0:T(256)}, u32[]{:S(2)}) copy-start(f32[256]{0:T(256)} %param.28) | copy-start | bytes 3076
  11.5 18.5 %copy-start = (bf16[2,512,512]{2,1,0:T(8,128)(2,1)S(1)}, bf16[2,512,512]{2,1,0:T(8,128)(2,1)}, u32[]{:S(2)}) copy-start(bf16[2,512,512]{2,1,0:T(8,128)(2,1)} %up_s.3) | copy-start | bytes 3145732
  11.5 18.5 %copy-start.1 = (bf16[2,512,256]{2,1,0:T(8,128)(2,1)S(1)}, bf16[2,512,256]{2,1,0:T(8,128)(2,1)}, u32[]{:S(2)}) copy-start(bf16[2,512,256]{2,1,0:T(8,128)(2,1)} %up_u.3) | copy-start | bytes 1572868
  11.6 18.5 %copy-start.10 = (f32[2]{0:T(128)S(1)}, f32[2]{0:T(128)}, u32[]{:S(2)}) copy-start(f32[2]{0:T(128)} %upw_ref.1) | copy-start | bytes 28
  30.0 46.0 %copy-start.3 = (bf16[4,512,512]{2,1,0:T(8,128)(2,1)S(1)}, bf16[4,512,512]{2,1,0:T(8,128)(2,1)}, u32[]{:S(2)}) copy-start(bf16[4,512,512]{2,1,0:T(8,128)(2,1)} %leaf_s.3) | copy-start | bytes 6291460
  30.0 46.0 %copy-start.4 = (bf16[4,512,256]{2,1,0:T(8,128)(2,1)S(1)}, bf16[4,512,256]{2,1,0:T(8,128)(2,1)}, u32[]{:S(2)}) copy-start(bf16[4,512,256]{2,1,0:T(8,128)(2,1)} %leaf_u.3) | copy-start | bytes 3145732
  30.0 46.0 %copy-start.6 = (bf16[512,512]{1,0:T(8,128)(2,1)S(1)}, bf16[512,512]{1,0:T(8,128)(2,1)}, u32[]{:S(2)}) copy-start(bf16[512,512]{1,0:T(8,128)(2,1)} %root_cov_ref.1) | copy-start | bytes 1572868
  30.0 46.0 %copy-start.9 = (f32[512]{0:T(512)S(1)}, f32[512]{0:T(512)}, u32[]{:S(2)}) copy-start(f32[512]{0:T(512)} %param.29) | copy-start | bytes 6148

commit v3 on v2

--- a/solution.py
+++ b/solution.py
@@ -477,11 +477,21 @@
     )(total, weight, sc, cc)
 
 
+def hops(step):
+    return min(step, 4 - step)
+
+
+NEAR = sorted(
+    [(dy, dx) for dy in range(4) for dx in range(4) if dy or dx],
+    key=lambda step: hops(step[0]) + hops(step[1]),
+)
+
+
 def root_kernel(
     upw_ref, gv_ref, up_s, up_u, gvs_ref, total_ref, wtiles_ref,
     term_ref, wtile_ref, in_buf, piece_buf, pair_buf,
-    w_send, w_recv, a_send, a_recv, b_send, b_recv, c_send, c_recv, s_send, s_recv,
-    g_send, g_recv, gs_send, gs_recv,
+    w_send, w_recv, ws_send, ws_recv, a_send, a_recv, b_send, b_recv, c_send, c_recv,
+    s_send, s_recv, g_send, g_recv, gs_send, gs_recv,
 ):
     row = lax.axis_index("row")
     col = lax.axis_index("col")
@@ -490,105 +500,16 @@
     sibling = col + 1 - 2 * core
     dist = lax.rem(z + 8 - 4 * core, 8)
     is_target = dist == 0
+    is_adder = dist == 4
+    is_plain = jnp.logical_not(jnp.logical_or(is_target, is_adder))
+    up_col = 2 * lax.rem(z + 1, 8) + core
+    down_col = 2 * lax.rem(z + 7, 8) + core
+    other_adder = 2 * lax.rem(z + 4, 8) + 1 - core
+    slot = 1 - core
     barrier = pltpu.get_barrier_semaphore()
 
-    def greet(k, carry):
-        pl.semaphore_signal(
-            barrier, inc=1, device_id=(row, lax.rem(col + k, 16)), device_id_type=MESH
-        )
-        pl.semaphore_signal(
-            barrier, inc=1, device_id=(lax.rem(row + k, 16), col), device_id_type=MESH
-        )
-        return carry
-
-    lax.fori_loop(1, 16, greet, 0)
-    wtile_ref[...] = jnp.full((8, 128), upw_ref[0] + upw_ref[1], F32)
-
-    @pl.when(is_target)
-    def _():
-        gvs_ref[pl.ds(core, 1)] = gv_ref[...][None]
-        up_weight = jnp.where(core == 0, upw_ref[0], upw_ref[1])
-
-        def put(i, block):
-            term_ref[i * H : (i + 1) * H, :] = (up_weight * block).astype(BF16)
-
-        node_term(gv_ref.at[pl.ds(NU, NX)], up_s.at[core], up_u.at[core], put)
-
-    pl.semaphore_wait(barrier, 30)
-
-    def a_copy(to_row, at):
-        return pltpu.make_async_remote_copy(
-            src_ref=term_ref.at[pl.ds(pl.multiple_of(to_row * PIECE, 16), PIECE)],
-            dst_ref=in_buf.at[at],
-            send_sem=a_send.at[to_row],
-            recv_sem=a_recv.at[at],
-            device_id=(to_row, col),
-            device_id_type=MESH,
-        )
-
-    def b_copy(to_col, slot):
-        half = lax.rem(to_col, 2)
-        return pltpu.make_async_remote_copy(
-            src_ref=piece_buf.at[half],
-            dst_ref=pair_buf.at[slot],
-            send_sem=b_send.at[to_col],
-            recv_sem=b_recv.at[slot],
-            device_id=(row, to_col),
-            device_id_type=MESH,
-        )
-
-    def c_copy(to_row, at):
-        return pltpu.make_async_remote_copy(
-            src_ref=total_ref.at[at, core],
-            dst_ref=total_ref.at[at, core],
-            send_sem=c_send.at[to_row],
-            recv_sem=c_recv.at[at],
-            device_id=(to_row, col),
-            device_id_type=MESH,
-        )
-
-    def s_copy(at, half):
-        return pltpu.make_async_remote_copy(
-            src_ref=total_ref.at[at, half],
-            dst_ref=total_ref.at[at, half],
-            send_sem=s_send.at[at],
-            recv_sem=s_recv.at[at],
-            device_id=(row, sibling),
-            device_id_type=MESH,
-        )
-
-    def w_copy(to_row, at):
-        return pltpu.make_async_remote_copy(
-            src_ref=wtile_ref,
-            dst_ref=wtiles_ref.at[at],
-            send_sem=w_send.at[to_row],
-            recv_sem=w_recv.at[at],
-            device_id=(to_row, col),
-            device_id_type=MESH,
-        )
-
-    def g_rows(c):
-        return pl.ds(pl.multiple_of(c * GV_CHUNK, 16), GV_CHUNK)
-
-    def g_copy(c, slot, to_col, lane_id):
-        return pltpu.make_async_remote_copy(
-            src_ref=gvs_ref.at[slot, g_rows(c)],
-            dst_ref=gvs_ref.at[slot, g_rows(c)],
-            send_sem=g_send.at[lane_id, c],
-            recv_sem=g_recv.at[c],
-            device_id=(row, to_col),
-            device_id_type=MESH,
-        )
-
-    def gs_copy(c, slot):
-        return pltpu.make_async_remote_copy(
-            src_ref=gvs_ref.at[slot, g_rows(c)],
-            dst_ref=gvs_ref.at[slot, g_rows(c)],
-            send_sem=gs_send.at[c],
-            recv_sem=gs_recv.at[c],
-            device_id=(row, sibling),
-            device_id_type=MESH,
-        )
+    def signal(to_row, to_col):
+        pl.semaphore_signal(barrier, inc=1, device_id=(to_row, to_col), device_id_type=MESH)
 
     def peers(body):
         def one(k, carry):
@@ -597,12 +518,115 @@
 
         lax.fori_loop(1, 16, one, 0)
 
-    def columns(body):
-        def one(k, carry):
-            body(lax.rem(col + k, 16))
-            return carry
-
-        lax.fori_loop(1, 16, one, 0)
+    def at_step(step):
+        return lax.rem(row // 4 + step[0], 4) * 4 + lax.rem(lax.rem(row, 4) + step[1], 4)
+
+    def far_first(body):
+        for step in reversed(NEAR):
+            body(at_step(step))
+
+    def near_first(body):
+        for step in NEAR:
+            body(at_step(step))
+
+    for to_col in (sibling, up_col, down_col):
+        signal(row, to_col)
+
+    @pl.when(is_target)
+    def _():
+        peers(lambda p: signal(p, sibling))
+
+    @pl.when(is_adder)
+    def _():
+        peers(lambda p: signal(p, sibling))
+        peers(lambda p: signal(p, col))
+        signal(row, other_adder)
+        for off in (1, 2, 3, 5, 6, 7):
+            for half in range(2):
+                signal(row, 2 * lax.rem(z + off, 8) + half)
+
+    @pl.when(is_plain)
+    def _():
+        peers(lambda p: signal(p, col))
+        signal(row, 1)
+        signal(row, 8)
+
+    wtile_ref[...] = jnp.full((8, 128), upw_ref[0] + upw_ref[1], F32)
+
+    @pl.when(is_target)
+    def _():
+        gvs_ref[pl.ds(core, 1)] = gv_ref[...][None]
+        up_weight = jnp.where(core == 0, upw_ref[0], upw_ref[1])
+
+        def put(i, block):
+            term_ref[i * H : (i + 1) * H, :] = (up_weight * block).astype(BF16)
+
+        node_term(gv_ref.at[pl.ds(NU, NX)], up_s.at[core], up_u.at[core], put)
+        pl.semaphore_wait(barrier, 18)
+
+    @pl.when(is_adder)
+    def _():
+        pl.semaphore_wait(barrier, 46)
+
+    @pl.when(is_plain)
+    def _():
+        pl.semaphore_wait(barrier, 20)
+
+    def remote(src, dst, send, recv, to_row, to_col):
+        return pltpu.make_async_remote_copy(
+            src_ref=src, dst_ref=dst, send_sem=send, recv_sem=recv,
+            device_id=(to_row, to_col), device_id_type=MESH,
+        )
+
+    def a_copy(to_row, at):
+        return remote(
+            term_ref.at[pl.ds(pl.multiple_of(to_row * PIECE, 16), PIECE)], in_buf.at[at],
+            a_send.at[to_row], a_recv.at[at], to_row, sibling,
+        )
+
+    def b_half(off, half, of_slot):
+        return remote(
+            piece_buf.at[half], pair_buf.at[of_slot, half],
+            b_send.at[2 * off + half], b_recv.at[of_slot], row, 2 * lax.rem(z + off, 8) + half,
+        )
+
+    def b_whole(of_slot):
+        return remote(
+            piece_buf, pair_buf.at[of_slot], b_send.at[0], b_recv.at[of_slot], row, other_adder
+        )
+
+    def c_half(to_row, at):
+        part = total_ref.at[at, core]
+        return remote(part, part, c_send.at[to_row], c_recv.at[at], to_row, col)
+
+    def c_whole(to_row, at):
+        part = total_ref.at[at]
+        return remote(part, part, c_send.at[to_row], c_recv.at[at], to_row, col)
+
+    def s_half(at, half):
+        part = total_ref.at[at, half]
+        return remote(part, part, s_send.at[at], s_recv.at[at], row, sibling)
+
+    def s_whole(at):
+        part = total_ref.at[at]
+        return remote(part, part, s_send.at[at], s_recv.at[at], row, sibling)
+
+    def w_copy(to_row, at):
+        return remote(wtile_ref, wtiles_ref.at[at], w_send.at[to_row], w_recv.at[at], to_row, col)
+
+    def ws_copy():
+        return remote(wtiles_ref, wtiles_ref, ws_send.at[0], ws_recv.at[0], row, sibling)
+
+    def g_part(c, of_slot):
+        return gvs_ref.at[of_slot, pl.ds(pl.multiple_of(c * GV_CHUNK, 16), GV_CHUNK)]
+
+    def g_copy(c, to_col, way):
+        part = g_part(c, core)
+        return remote(part, part, g_send.at[way, c], g_recv.at[c], row, to_col)
+
+    def gs_copy(c, of_slot):
+        part = g_part(c, of_slot)
+        return remote(part, part, gs_send.at[c], gs_recv.at[c], row, sibling)
 
     def gv_chunks(body, first=0, last=N_GV):
         def one(c, carry):
@@ -611,93 +635,113 @@
 
         lax.fori_loop(first, last, one, 0)
 
-    up_col = 2 * lax.rem(z + 1, 8) + core
-    down_col = 2 * lax.rem(z + 7, 8) + core
     to_up = dist <= 3
     to_down = jnp.logical_or(dist == 0, dist >= 6)
 
     def forward(c):
         @pl.when(to_up)
         def _():
-            g_copy(c, core, up_col, 0).start()
+            g_copy(c, up_col, 0).start()
 
         @pl.when(to_down)
         def _():
-            g_copy(c, core, down_col, 1).start()
+            g_copy(c, down_col, 1).start()
 
         gs_copy(c, core).start()
 
+    def relay(c):
+        g_copy(c, up_col, 0).wait_recv()
+        forward(c)
+
+    def pieces(body):
+        def one(at, carry):
+            body(at)
+            return carry
+
+        lax.fori_loop(0, 16, one, 0)
+
+    def send_tiles():
+        peers(lambda p: w_copy(p, row).start())
+        wtiles_ref[pl.ds(row, 1)] = wtile_ref[...][None]
+
     @pl.when(is_target)
     def _():
-        peers(lambda p: a_copy(p, row).start())
-
-    peers(lambda p: w_copy(p, row).start())
-
-    @pl.when(is_target)
-    def _():
+        far_first(lambda p: a_copy(p, row).start())
+        a_copy(row, row).start()
         gv_chunks(forward)
-        acc = term_ref[pl.ds(pl.multiple_of(row * PIECE, 16), PIECE), :].astype(F32)
-
-        def add(k, acc):
-            source = lax.rem(row + k, 16)
+        pieces(lambda at: s_whole(at).wait_recv())
+        ws_copy().wait_recv()
+        pieces(lambda p: a_copy(p, row).wait_send())
+
+    @pl.when(is_adder)
+    def _():
+        send_tiles()
+        a_copy(row, row).wait_recv()
+        acc = in_buf[row].astype(F32)
+        for step in NEAR:
+            source = at_step(step)
             a_copy(source, source).wait_recv()
-            return acc + in_buf[source].astype(F32)
-
-        acc = lax.fori_loop(1, 16, add, acc)
+            acc = acc + in_buf[source].astype(F32)
         piece = acc.astype(BF16)
         piece_buf[0] = piece[:HALF]
         piece_buf[1] = piece[HALF:]
-        columns(lambda p: b_copy(p, core).start())
-        pair_buf[pl.ds(core, 1)] = piece_buf[pl.ds(core, 1)]
-        b_copy(col, 1 - core).wait_recv()
-
-    def relay(c):
-        g_copy(c, core, up_col, 0).wait_recv()
-        forward(c)
-
-    hops = jnp.minimum(dist, 8 - dist)
-    early = jnp.where(hops <= 2, N_GV, jnp.where(hops == 3, N_GV // 2, 0))
-
-    @pl.when(jnp.logical_not(is_target))
-    def _():
+        b_whole(slot).start()
+        for off in (3, 5, 2, 6, 1, 7):
+            for half in range(2):
+                b_half(off, half, slot).start()
+        own = piece_buf[...].astype(F32)
+        b_whole(core).wait_recv()
+        pair = own + pair_buf[core].astype(F32)
+        total_ref[pl.ds(row, 1)] = pair.astype(BF16)[None]
+        far_first(lambda p: c_whole(p, row).start())
+        s_whole(row).start()
+        gv_chunks(relay)
+
+        def relay_piece(p):
+            c_whole(p, p).wait_recv()
+            s_whole(p).start()
+
+        near_first(relay_piece)
+        peers(lambda p: w_copy(p, p).wait_recv())
+        ws_copy().start()
+        ws_copy().wait_send()
+        pieces(lambda at: s_whole(at).wait_send())
+        peers(lambda p: c_whole(p, row).wait_send())
+        peers(lambda p: w_copy(p, row).wait_send())
+        b_whole(slot).wait_send()
+        for off in (3, 5, 2, 6, 1, 7):
+            for half in range(2):
+                b_half(off, half, slot).wait_send()
+
+    steps = jnp.minimum(dist, 8 - dist)
+    early = jnp.where(steps <= 2, N_GV, N_GV // 2)
+
+    @pl.when(is_plain)
+    def _():
+        send_tiles()
         gv_chunks(relay, 0, early)
-        b_copy(col, 0).wait_recv()
-        b_copy(col, 1).wait_recv()
-
-    pair = pair_buf[0].astype(F32) + pair_buf[1].astype(F32)
-    total_ref[pl.ds(row, 1), pl.ds(core, 1)] = pair.astype(BF16)[None, None]
-    peers(lambda p: c_copy(p, row).start())
-    s_copy(row, core).start()
-
-    @pl.when(jnp.logical_not(is_target))
-    def _():
+        b_half(1, core, 0).wait_recv()
+        b_half(1, core, 1).wait_recv()
+        pair = pair_buf[0, core].astype(F32) + pair_buf[1, core].astype(F32)
+        total_ref[pl.ds(row, 1), pl.ds(core, 1)] = pair.astype(BF16)[None, None]
+        far_first(lambda p: c_half(p, row).start())
+        s_half(row, core).start()
         gv_chunks(relay, early, N_GV)
 
-    def relay_piece(p):
-        c_copy(p, p).wait_recv()
-        s_copy(p, core).start()
-
-    peers(relay_piece)
-
-    def finish(at, carry):
-        s_copy(at, 1 - core).wait_recv()
-        s_copy(at, core).wait_send()
-        return carry
-
-    lax.fori_loop(0, 16, finish, 0)
-
-    def finish_peer(p):
-        c_copy(p, row).wait_send()
-        w_copy(p, row).wait_send()
-        w_copy(p, p).wait_recv()
-
-    peers(finish_peer)
-    wtiles_ref[pl.ds(row, 1)] = wtile_ref[...][None]
-
-    @pl.when(is_target)
-    def _():
-        peers(lambda p: a_copy(p, row).wait_send())
-        columns(lambda p: b_copy(p, core).wait_send())
+        def relay_piece(p):
+            c_half(p, p).wait_recv()
+            s_half(p, core).start()
+
+        near_first(relay_piece)
+
+        def finish(at):
+            s_half(at, 1 - core).wait_recv()
+            s_half(at, core).wait_send()
+
+        pieces(finish)
+        peers(lambda p: w_copy(p, p).wait_recv())
+        peers(lambda p: c_half(p, row).wait_send())
+        peers(lambda p: w_copy(p, row).wait_send())
 
     def finish_gv(c):
         gs_copy(c, 1 - core).wait_recv()
@@ -705,11 +749,11 @@
 
         @pl.when(to_up)
         def _():
-            g_copy(c, core, up_col, 0).wait_send()
+            g_copy(c, up_col, 0).wait_send()
 
         @pl.when(to_down)
         def _():
-            g_copy(c, core, down_col, 1).wait_send()
+            g_copy(c, down_col, 1).wait_send()
 
     gv_chunks(finish_gv)
 
@@ -732,8 +776,9 @@
             pltpu.VMEM((8, 128), F32),
             pltpu.VMEM((16, PIECE, H), BF16),
             pltpu.VMEM((2, HALF, H), BF16),
-            pltpu.VMEM((2, HALF, H), BF16),
+            pltpu.VMEM((2, 2, HALF, H), BF16),
             dma((16,)), dma((16,)),
+            dma((1,)), dma((1,)),
             dma((16,)), dma((16,)),
             dma((16,)), dma((2,)),
             dma((16,)), dma((16,)),

time: 86.7 us -> 83.8 us (0.967); the launches traced: 86.6 us -> 82.7 us
  Pallas kernels: 83.6 us -> 79.7 us
    pallas_call x1, Pallas kernels: 45.9 us -> 42.5 us  [root_sum(): pl.pallas_call(root_kernel, out_shape=(jax.ShapeDtypeStruct((2, GV_ROWS,...]
where the time goes in v3:
time: 83.8 us; the launch traced here: 82.7 us
  Pallas kernels  79.7 us (95%)
  between operations  2.95 us (4%)
    pallas_call x1, Pallas kernels, root_sum(): pl.pallas_call(root_kernel, out_shape=(jax.ShapeDtypeStruct((2, GV_ROWS,...  42.5 us
    pallas_call x1, Pallas kernels, gather(): pl.pallas_call(gather_kernel, out_shape=(jax.ShapeDtypeStruct((ROWS, H),...  18.7 us
    pallas_call x1, Pallas kernels, down(): pl.pallas_call(down_kernel, out_shape=(jax.ShapeDtypeStruct((NU, NX), BF1...  10.3 us
    pallas_call x1, Pallas kernels, lower(): pl.pallas_call(lower_kernel, out_shape=(jax.ShapeDtypeStruct((NU, NX), BF...  8.1 us

profile of v3, /device:TPU:1, one launch (start us, length us, event | category | flops | bytes accessed | tf_op | source)
XLA Modules:
  0.0 82.7 jit_solution(461764186595144048)
XLA Ops:
  2.6 0.0 copy-start.2
  2.6 0.0 copy-start.5
  2.6 0.0 copy-start.7
  2.6 0.0 copy-start.8
  2.6 8.1 %lower_nodes.1 = (bf16[256,512]{1,0:T(8,128)(2,1)S(1)}, bf16[512,512]{1,0:T(8,128)(2,1)S(1)}) custom-call(s32[1]{0:T(128)S(6)} %copy.24.count_ref, bf16[4,512,512]{2,1,0:T(8,128)(2,1)} %leaf_s.3, bf16[4,512,256]{2,1,0:T(8,128)(2,1)} %leaf_u.3, bf16[1,4]{1,0:T(2,128)(2,1)} %bitcast.19, f32[1,512]{1,0:T(1,128)} %bitcast.9, f32[1,256]{1,0:T(1,128)} %bitcast.12), custom_call_target="tpu_custom_call" | custom-call | flops 2415919104 | bytes 3145728 | tf_op jit(solution)/shard_map/lower_nodes/pallas_call | solution.py:247
  10.7 0.0 copy-start
  10.7 0.0 copy-start.1
  10.8 0.0 copy-start.10
  10.8 0.0 copy-done.2
  10.8 0.0 copy-done.5
  10.8 18.7 %group_sum.1 = (f32[1536,256]{1,0:T(8,128)S(1)}, f32[8,128]{1,0:T(8,128)S(1)}) custom-call(s32[1]{0:T(128)S(6)} %copy.26.parent_ref, f32[1]{0:T(128)S(6)} %copy.25.midw_ref, bf16[512,512]{1,0:T(8,128)(2,1)S(1)} %get-tuple-element.25.value_ref.mid_value_ref, bf16[1,512,512]{2,1,0:T(8,128)(2,1)S(1)} %copy-done.2, bf16[1,512,256]{2,1,0:T(8,128)(2,1)S(1)} %copy-done.5), custom_call_target="tpu_custom_call" | custom-call | tf_op jit(solution)/shard_map/group_sum/pallas_call | solution.py:418
  29.5 0.0 copy-done.7
  29.5 0.0 copy-done.8
  29.6 0.0 copy-start.3
  29.6 0.0 copy-start.4
  29.6 0.0 copy-start.6
  29.6 0.0 copy-start.9
  29.6 0.0 copy-done
  29.6 0.0 copy-done.1
  29.6 0.0 copy-done.10
  29.7 42.5 %root_sum.1 = (bf16[2,768,512]{2,1,0:T(8,128)(2,1)S(1)}, bf16[16,2,48,256]{3,2,1,0:T(8,128)(2,1)S(1)}, f32[16,8,128]{2,1,0:T(8,128)S(1)}) custom-call(f32[2]{0:T(128)S(1)} %copy-done.10, bf16[768,512]{1,0:T(8,128)(2,1)S(1)} %upper_nodes.1.gv_ref, bf16[2,512,512]{2,1,0:T(8,128)(2,1)S(1)} %copy-done, bf16[2,512,256]{2,1,0:T(8,128)(2,1)S(1)} %copy-done.1), custom_call_target="tpu_custom_call" | custom-call | tf_op jit(solution)/shard_map/root_sum/pallas_call | solution.py:765
  72.2 0.0 copy-done.3
  72.2 0.0 copy-done.4
  72.2 0.0 copy-done.6
  72.2 0.0 copy-done.9
  72.2 10.3 %down_sweep.1 = (bf16[256,512]{1,0:T(8,128)(2,1)}, bf16[512,512]{1,0:T(8,128)(2,1)}, bf16[2,256,512]{2,1,0:T(8,128)(2,1)}, bf16[2,512,512]{2,1,0:T(8,128)(2,1)},...) custom-call(s32[1]{0:T(128)S(6)} %copy.24.count_ref, ...), custom_call_target="tpu_custom_call" | custom-call | tf_op jit(solution)/shard_map/down_sweep/pallas_call | solution.py:852
  (1 shorter events, 0.0 us)
Async XLA Ops:
  2.6 8.2 %copy-start.2 = (bf16[1,512,512]{2,1,0:T(8,128)(2,1)S(1)}, bf16[1,512,512]{2,1,0:T(8,128)(2,1)}, u32[]{:S(2)}) copy-start(bf16[1,512,512]{2,1,0:T(8,128)(2,1)} %mid_s.3) | copy-start | bytes 1572868
  2.6 8.2 %copy-start.5 = (bf16[1,512,256]{2,1,0:T(8,128)(2,1)S(1)}, bf16[1,512,256]{2,1,0:T(8,128)(2,1)}, u32[]{:S(2)}) copy-start(bf16[1,512,256]{2,1,0:T(8,128)(2,1)} %mid_u.3) | copy-start | bytes 786436
  2.6 26.9 %copy-start.7 = (f32[512]{0:T(512)S(1)}, f32[512]{0:T(512)}, u32[]{:S(2)}) copy-start(f32[512]{0:T(512)} %param.27) | copy-start | bytes 6148
  2.6 26.9 %copy-start.8 = (f32[256]{0:T(256)S(1)}, f32[256]{0:T(256)}, u32[]{:S(2)}) copy-start(f32[256]{0:T(256)} %param.28) | copy-start | bytes 3076
  10.7 18.9 %copy-start = (bf16[2,512,512]{2,1,0:T(8,128)(2,1)S(1)}, bf16[2,512,512]{2,1,0:T(8,128)(2,1)}, u32[]{:S(2)}) copy-start(bf16[2,512,512]{2,1,0:T(8,128)(2,1)} %up_s.3) | copy-start | bytes 3145732
  10.7 18.9 %copy-start.1 = (bf16[2,512,256]{2,1,0:T(8,128)(2,1)S(1)}, bf16[2,512,256]{2,1,0:T(8,128)(2,1)}, u32[]{:S(2)}) copy-start(bf16[2,512,256]{2,1,0:T(8,128)(2,1)} %up_u.3) | copy-start | bytes 1572868
  10.8 18.9 %copy-start.10 = (f32[2]{0:T(128)S(1)}, f32[2]{0:T(128)}, u32[]{:S(2)}) copy-start(f32[2]{0:T(128)} %upw_ref.1) | copy-start | bytes 28
  29.6 42.6 %copy-start.3 = (bf16[4,512,512]{2,1,0:T(8,128)(2,1)S(1)}, bf16[4,512,512]{2,1,0:T(8,128)(2,1)}, u32[]{:S(2)}) copy-start(bf16[4,512,512]{2,1,0:T(8,128)(2,1)} %leaf_s.3) | copy-start | bytes 6291460
  29.6 42.6 %copy-start.4 = (bf16[4,512,256]{2,1,0:T(8,128)(2,1)S(1)}, bf16[4,512,256]{2,1,0:T(8,128)(2,1)}, u32[]{:S(2)}) copy-start(bf16[4,512,256]{2,1,0:T(8,128)(2,1)} %leaf_u.3) | copy-start | bytes 3145732
  29.6 42.6 %copy-start.6 = (bf16[512,512]{1,0:T(8,128)(2,1)S(1)}, bf16[512,512]{1,0:T(8,128)(2,1)}, u32[]{:S(2)}) copy-start(bf16[512,512]{1,0:T(8,128)(2,1)} %root_cov_ref.1) | copy-start | bytes 1572868
  29.6 42.6 %copy-start.9 = (f32[512]{0:T(512)S(1)}, f32[512]{0:T(512)}, u32[]{:S(2)}) copy-start(f32[512]{0:T(512)} %param.29) | copy-start | bytes 6148

commit v4 on v3

--- a/solution.py
+++ b/solution.py
@@ -551,27 +551,6 @@
         signal(row, 1)
         signal(row, 8)
 
-    wtile_ref[...] = jnp.full((8, 128), upw_ref[0] + upw_ref[1], F32)
-
-    @pl.when(is_target)
-    def _():
-        gvs_ref[pl.ds(core, 1)] = gv_ref[...][None]
-        up_weight = jnp.where(core == 0, upw_ref[0], upw_ref[1])
-
-        def put(i, block):
-            term_ref[i * H : (i + 1) * H, :] = (up_weight * block).astype(BF16)
-
-        node_term(gv_ref.at[pl.ds(NU, NX)], up_s.at[core], up_u.at[core], put)
-        pl.semaphore_wait(barrier, 18)
-
-    @pl.when(is_adder)
-    def _():
-        pl.semaphore_wait(barrier, 46)
-
-    @pl.when(is_plain)
-    def _():
-        pl.semaphore_wait(barrier, 20)
-
     def remote(src, dst, send, recv, to_row, to_col):
         return pltpu.make_async_remote_copy(
             src_ref=src, dst_ref=dst, send_sem=send, recv_sem=recv,
@@ -664,11 +643,32 @@
         peers(lambda p: w_copy(p, row).start())
         wtiles_ref[pl.ds(row, 1)] = wtile_ref[...][None]
 
+    wtile_ref[...] = jnp.full((8, 128), upw_ref[0] + upw_ref[1], F32)
+
     @pl.when(is_target)
     def _():
+        gvs_ref[pl.ds(core, 1)] = gv_ref[...][None]
+        up_weight = jnp.where(core == 0, upw_ref[0], upw_ref[1])
+        pl.semaphore_wait(barrier, 18)
+        gv_chunks(forward)
+
+        def put(i, block):
+            term_ref[i * H : (i + 1) * H, :] = (up_weight * block).astype(BF16)
+
+        node_term(gv_ref.at[pl.ds(NU, NX)], up_s.at[core], up_u.at[core], put)
         far_first(lambda p: a_copy(p, row).start())
         a_copy(row, row).start()
-        gv_chunks(forward)
+
+    @pl.when(is_adder)
+    def _():
+        pl.semaphore_wait(barrier, 46)
+
+    @pl.when(is_plain)
+    def _():
+        pl.semaphore_wait(barrier, 20)
+
+    @pl.when(is_target)
+    def _():
         pieces(lambda at: s_whole(at).wait_recv())
         ws_copy().wait_recv()
         pieces(lambda p: a_copy(p, row).wait_send())
@@ -695,13 +695,12 @@
         total_ref[pl.ds(row, 1)] = pair.astype(BF16)[None]
         far_first(lambda p: c_whole(p, row).start())
         s_whole(row).start()
-        gv_chunks(relay)
-
         def relay_piece(p):
             c_whole(p, p).wait_recv()
             s_whole(p).start()
 
         near_first(relay_piece)
+        gv_chunks(relay)
         peers(lambda p: w_copy(p, p).wait_recv())
         ws_copy().start()
         ws_copy().wait_send()

time: 83.8 us -> 82.5 us (0.984); the launches traced: 82.7 us -> 82.3 us
  no operation moved by 1% of the time
where the time goes in v4:
time: 82.5 us; the launch traced here: 82.3 us
  Pallas kernels  79.3 us (96%)
  between operations  2.95 us (4%)
    pallas_call x1, Pallas kernels, root_sum(): pl.pallas_call(root_kernel, out_shape=(jax.ShapeDtypeStruct((2, GV_ROWS,...  41.7 us
    pallas_call x1, Pallas kernels, gather(): pl.pallas_call(gather_kernel, out_shape=(jax.ShapeDtypeStruct((ROWS, H),...  18.4 us
    pallas_call x1, Pallas kernels, down(): pl.pallas_call(down_kernel, out_shape=(jax.ShapeDtypeStruct((NU, NX), BF1...  10.3 us
    pallas_call x1, Pallas kernels, lower(): pl.pallas_call(lower_kernel, out_shape=(jax.ShapeDtypeStruct((NU, NX), BF...  8.9 us

profile of v4, /device:TPU:1, one launch (start us, length us, event | category | flops | bytes accessed | tf_op | source)
XLA Modules:
  0.0 82.3 jit_solution(6734760008356625989)
XLA Ops:
  2.6 0.0 copy-start.2
  2.6 0.0 copy-start.5
  2.6 0.0 copy-start.7
  2.6 0.0 copy-start.8
  2.6 8.9 %lower_nodes.1 = (bf16[256,512]{1,0:T(8,128)(2,1)S(1)}, bf16[512,512]{1,0:T(8,128)(2,1)S(1)}) custom-call(s32[1]{0:T(128)S(6)} %copy.24.count_ref, bf16[4,512,512]{2,1,0:T(8,128)(2,1)} %leaf_s.3, bf16[4,512,256]{2,1,0:T(8,128)(2,1)} %leaf_u.3, bf16[1,4]{1,0:T(2,128)(2,1)} %bitcast.19, f32[1,512]{1,0:T(1,128)} %bitcast.9, f32[1,256]{1,0:T(1,128)} %bitcast.12), custom_call_target="tpu_custom_call" | custom-call | flops 2415919104 | bytes 3145728 | tf_op jit(solution)/shard_map/lower_nodes/pallas_call | solution.py:247
  11.5 0.0 copy-start
  11.5 0.0 copy-start.1
  11.6 0.0 copy-start.10
  11.6 0.0 copy-done.2
  11.6 0.0 copy-done.5
  11.6 18.4 %group_sum.1 = (f32[1536,256]{1,0:T(8,128)S(1)}, f32[8,128]{1,0:T(8,128)S(1)}) custom-call(s32[1]{0:T(128)S(6)} %copy.26.parent_ref, f32[1]{0:T(128)S(6)} %copy.25.midw_ref, bf16[512,512]{1,0:T(8,128)(2,1)S(1)} %get-tuple-element.25.value_ref.mid_value_ref, bf16[1,512,512]{2,1,0:T(8,128)(2,1)S(1)} %copy-done.2, bf16[1,512,256]{2,1,0:T(8,128)(2,1)S(1)} %copy-done.5), custom_call_target="tpu_custom_call" | custom-call | tf_op jit(solution)/shard_map/group_sum/pallas_call | solution.py:418
  29.9 0.0 copy-done.7
  30.0 0.0 copy-done.8
  30.0 0.0 copy-start.3
  30.0 0.0 copy-start.4
  30.0 0.0 copy-start.6
  30.0 0.0 copy-start.9
  30.0 0.0 copy-done
  30.0 0.0 copy-done.1
  30.1 0.0 copy-done.10
  30.1 41.7 %root_sum.1 = (bf16[2,768,512]{2,1,0:T(8,128)(2,1)S(1)}, bf16[16,2,48,256]{3,2,1,0:T(8,128)(2,1)S(1)}, f32[16,8,128]{2,1,0:T(8,128)S(1)}) custom-call(f32[2]{0:T(128)S(1)} %copy-done.10, bf16[768,512]{1,0:T(8,128)(2,1)S(1)} %upper_nodes.1.gv_ref, bf16[2,512,512]{2,1,0:T(8,128)(2,1)S(1)} %copy-done, bf16[2,512,256]{2,1,0:T(8,128)(2,1)S(1)} %copy-done.1), custom_call_target="tpu_custom_call" | custom-call | tf_op jit(solution)/shard_map/root_sum/pallas_call | solution.py:764
  71.8 0.0 copy-done.3
  71.8 0.0 copy-done.4
  71.8 0.0 copy-done.6
  71.8 0.0 copy-done.9
  71.8 10.3 %down_sweep.1 = (bf16[256,512]{1,0:T(8,128)(2,1)}, bf16[512,512]{1,0:T(8,128)(2,1)}, bf16[2,256,512]{2,1,0:T(8,128)(2,1)}, bf16[2,512,512]{2,1,0:T(8,128)(2,1)},...) custom-call(s32[1]{0:T(128)S(6)} %copy.24.count_ref, ...), custom_call_target="tpu_custom_call" | custom-call | tf_op jit(solution)/shard_map/down_sweep/pallas_call | solution.py:851
  (1 shorter events, 0.0 us)
Async XLA Ops:
  2.6 9.0 %copy-start.2 = (bf16[1,512,512]{2,1,0:T(8,128)(2,1)S(1)}, bf16[1,512,512]{2,1,0:T(8,128)(2,1)}, u32[]{:S(2)}) copy-start(bf16[1,512,512]{2,1,0:T(8,128)(2,1)} %mid_s.3) | copy-start | bytes 1572868
  2.6 9.0 %copy-start.5 = (bf16[1,512,256]{2,1,0:T(8,128)(2,1)S(1)}, bf16[1,512,256]{2,1,0:T(8,128)(2,1)}, u32[]{:S(2)}) copy-start(bf16[1,512,256]{2,1,0:T(8,128)(2,1)} %mid_u.3) | copy-start | bytes 786436
  2.6 27.3 %copy-start.7 = (f32[512]{0:T(512)S(1)}, f32[512]{0:T(512)}, u32[]{:S(2)}) copy-start(f32[512]{0:T(512)} %param.27) | copy-start | bytes 6148
  2.6 27.3 %copy-start.8 = (f32[256]{0:T(256)S(1)}, f32[256]{0:T(256)}, u32[]{:S(2)}) copy-start(f32[256]{0:T(256)} %param.28) | copy-start | bytes 3076
  11.5 18.5 %copy-start = (bf16[2,512,512]{2,1,0:T(8,128)(2,1)S(1)}, bf16[2,512,512]{2,1,0:T(8,128)(2,1)}, u32[]{:S(2)}) copy-start(bf16[2,512,512]{2,1,0:T(8,128)(2,1)} %up_s.3) | copy-start | bytes 3145732
  11.5 18.5 %copy-start.1 = (bf16[2,512,256]{2,1,0:T(8,128)(2,1)S(1)}, bf16[2,512,256]{2,1,0:T(8,128)(2,1)}, u32[]{:S(2)}) copy-start(bf16[2,512,256]{2,1,0:T(8,128)(2,1)} %up_u.3) | copy-start | bytes 1572868
  11.6 18.5 %copy-start.10 = (f32[2]{0:T(128)S(1)}, f32[2]{0:T(128)}, u32[]{:S(2)}) copy-start(f32[2]{0:T(128)} %upw_ref.1) | copy-start | bytes 28
  30.0 41.8 %copy-start.3 = (bf16[4,512,512]{2,1,0:T(8,128)(2,1)S(1)}, bf16[4,512,512]{2,1,0:T(8,128)(2,1)}, u32[]{:S(2)}) copy-start(bf16[4,512,512]{2,1,0:T(8,128)(2,1)} %leaf_s.3) | copy-start | bytes 6291460
  30.0 41.8 %copy-start.4 = (bf16[4,512,256]{2,1,0:T(8,128)(2,1)S(1)}, bf16[4,512,256]{2,1,0:T(8,128)(2,1)}, u32[]{:S(2)}) copy-start(bf16[4,512,256]{2,1,0:T(8,128)(2,1)} %leaf_u.3) | copy-start | bytes 3145732
  30.0 41.8 %copy-start.6 = (bf16[512,512]{1,0:T(8,128)(2,1)S(1)}, bf16[512,512]{1,0:T(8,128)(2,1)}, u32[]{:S(2)}) copy-start(bf16[512,512]{1,0:T(8,128)(2,1)} %root_cov_ref.1) | copy-start | bytes 1572868
  30.0 41.8 %copy-start.9 = (f32[512]{0:T(512)S(1)}, f32[512]{0:T(512)}, u32[]{:S(2)}) copy-start(f32[512]{0:T(512)} %param.29) | copy-start | bytes 6148

commit v5 on v4

--- a/solution.py
+++ b/solution.py
@@ -84,7 +84,7 @@
     error0 = rad * rad / den
     steps = jnp.int32(0)
     for j in range(16):
-        steps += (error0 > 0.1 ** (0.5**j)).astype(jnp.int32)
+        steps += (error0 > 0.3 ** (0.5**j)).astype(jnp.int32)
     h_hi, h_lo = split(hess)
     ba_hi, ba_lo = split(ba)
     work[...] = jnp.where(eye, 4.0 * mid / den, 0.0) - (2.0 / den) * hess

time: 82.5 us -> 81.3 us (0.985)
  Pallas kernels: 79.3 us -> 78 us
    pallas_call x1, Pallas kernels: 8.9 us -> 7.7 us  [lower(): pl.pallas_call(lower_kernel, out_shape=(jax.ShapeDtypeStruct((NU, NX), BF...]
where the time goes in v5:
time: 81.3 us; the launch traced here: 81 us
  Pallas kernels  78 us (96%)
  between operations  2.95 us (4%)
    pallas_call x1, Pallas kernels, root_sum(): pl.pallas_call(root_kernel, out_shape=(jax.ShapeDtypeStruct((2, GV_ROWS,...  41.2 us
    pallas_call x1, Pallas kernels, gather(): pl.pallas_call(gather_kernel, out_shape=(jax.ShapeDtypeStruct((ROWS, H),...  19.1 us
    pallas_call x1, Pallas kernels, down(): pl.pallas_call(down_kernel, out_shape=(jax.ShapeDtypeStruct((NU, NX), BF1...  9.94 us
    pallas_call x1, Pallas kernels, lower(): pl.pallas_call(lower_kernel, out_shape=(jax.ShapeDtypeStruct((NU, NX), BF...  7.7 us

profile of v5, /device:TPU:1, one launch (start us, length us, event | category | flops | bytes accessed | tf_op | source)
XLA Modules:
  0.0 81.0 jit_solution(14051055920862710399)
XLA Ops:
  2.6 0.0 copy-start.2
  2.6 0.0 copy-start.5
  2.6 0.0 copy-start.7
  2.6 0.0 copy-start.8
  2.6 7.7 %lower_nodes.1 = (bf16[256,512]{1,0:T(8,128)(2,1)S(1)}, bf16[512,512]{1,0:T(8,128)(2,1)S(1)}) custom-call(s32[1]{0:T(128)S(6)} %copy.24.count_ref, bf16[4,512,512]{2,1,0:T(8,128)(2,1)} %leaf_s.3, bf16[4,512,256]{2,1,0:T(8,128)(2,1)} %leaf_u.3, bf16[1,4]{1,0:T(2,128)(2,1)} %bitcast.19, f32[1,512]{1,0:T(1,128)} %bitcast.9, f32[1,256]{1,0:T(1,128)} %bitcast.12), custom_call_target="tpu_custom_call" | custom-call | flops 2415919104 | bytes 3145728 | tf_op jit(solution)/shard_map/lower_nodes/pallas_call | solution.py:247
  10.3 0.0 copy-start
  10.3 0.0 copy-start.1
  10.3 0.0 copy-start.10
  10.4 0.0 copy-done.2
  10.4 0.0 copy-done.5
  10.4 19.1 %group_sum.1 = (f32[1536,256]{1,0:T(8,128)S(1)}, f32[8,128]{1,0:T(8,128)S(1)}) custom-call(s32[1]{0:T(128)S(6)} %copy.26.parent_ref, f32[1]{0:T(128)S(6)} %copy.25.midw_ref, bf16[512,512]{1,0:T(8,128)(2,1)S(1)} %get-tuple-element.25.value_ref.mid_value_ref, bf16[1,512,512]{2,1,0:T(8,128)(2,1)S(1)} %copy-done.2, bf16[1,512,256]{2,1,0:T(8,128)(2,1)S(1)} %copy-done.5), custom_call_target="tpu_custom_call" | custom-call | tf_op jit(solution)/shard_map/group_sum/pallas_call | solution.py:418
  29.5 0.0 copy-done.7
  29.5 0.0 copy-done.8
  29.6 0.0 copy-start.3
  29.6 0.0 copy-start.4
  29.6 0.0 copy-start.6
  29.6 0.0 copy-start.9
  29.6 0.0 copy-done
  29.6 0.0 copy-done.1
  29.6 0.0 copy-done.10
  29.7 41.2 %root_sum.1 = (bf16[2,768,512]{2,1,0:T(8,128)(2,1)S(1)}, bf16[16,2,48,256]{3,2,1,0:T(8,128)(2,1)S(1)}, f32[16,8,128]{2,1,0:T(8,128)S(1)}) custom-call(f32[2]{0:T(128)S(1)} %copy-done.10, bf16[768,512]{1,0:T(8,128)(2,1)S(1)} %upper_nodes.1.gv_ref, bf16[2,512,512]{2,1,0:T(8,128)(2,1)S(1)} %copy-done, bf16[2,512,256]{2,1,0:T(8,128)(2,1)S(1)} %copy-done.1), custom_call_target="tpu_custom_call" | custom-call | tf_op jit(solution)/shard_map/root_sum/pallas_call | solution.py:764
  70.9 0.0 copy-done.3
  70.9 0.0 copy-done.4
  70.9 0.0 copy-done.6
  70.9 0.0 copy-done.9
  70.9 9.9 %down_sweep.1 = (bf16[256,512]{1,0:T(8,128)(2,1)}, bf16[512,512]{1,0:T(8,128)(2,1)}, bf16[2,256,512]{2,1,0:T(8,128)(2,1)}, bf16[2,512,512]{2,1,0:T(8,128)(2,1)},...) custom-call(s32[1]{0:T(128)S(6)} %copy.24.count_ref, ...), custom_call_target="tpu_custom_call" | custom-call | tf_op jit(solution)/shard_map/down_sweep/pallas_call | solution.py:851
  (1 shorter events, 0.0 us)
Async XLA Ops:
  2.6 7.8 %copy-start.2 = (bf16[1,512,512]{2,1,0:T(8,128)(2,1)S(1)}, bf16[1,512,512]{2,1,0:T(8,128)(2,1)}, u32[]{:S(2)}) copy-start(bf16[1,512,512]{2,1,0:T(8,128)(2,1)} %mid_s.3) | copy-start | bytes 1572868
  2.6 7.8 %copy-start.5 = (bf16[1,512,256]{2,1,0:T(8,128)(2,1)S(1)}, bf16[1,512,256]{2,1,0:T(8,128)(2,1)}, u32[]{:S(2)}) copy-start(bf16[1,512,256]{2,1,0:T(8,128)(2,1)} %mid_u.3) | copy-start | bytes 786436
  2.6 26.9 %copy-start.7 = (f32[512]{0:T(512)S(1)}, f32[512]{0:T(512)}, u32[]{:S(2)}) copy-start(f32[512]{0:T(512)} %param.27) | copy-start | bytes 6148
  2.6 26.9 %copy-start.8 = (f32[256]{0:T(256)S(1)}, f32[256]{0:T(256)}, u32[]{:S(2)}) copy-start(f32[256]{0:T(256)} %param.28) | copy-start | bytes 3076
  10.3 19.3 %copy-start = (bf16[2,512,512]{2,1,0:T(8,128)(2,1)S(1)}, bf16[2,512,512]{2,1,0:T(8,128)(2,1)}, u32[]{:S(2)}) copy-start(bf16[2,512,512]{2,1,0:T(8,128)(2,1)} %up_s.3) | copy-start | bytes 3145732
  10.3 19.3 %copy-start.1 = (bf16[2,512,256]{2,1,0:T(8,128)(2,1)S(1)}, bf16[2,512,256]{2,1,0:T(8,128)(2,1)}, u32[]{:S(2)}) copy-start(bf16[2,512,256]{2,1,0:T(8,128)(2,1)} %up_u.3) | copy-start | bytes 1572868
  10.3 19.3 %copy-start.10 = (f32[2]{0:T(128)S(1)}, f32[2]{0:T(128)}, u32[]{:S(2)}) copy-start(f32[2]{0:T(128)} %upw_ref.1) | copy-start | bytes 28
  29.6 41.4 %copy-start.3 = (bf16[4,512,512]{2,1,0:T(8,128)(2,1)S(1)}, bf16[4,512,512]{2,1,0:T(8,128)(2,1)}, u32[]{:S(2)}) copy-start(bf16[4,512,512]{2,1,0:T(8,128)(2,1)} %leaf_s.3) | copy-start | bytes 6291460
  29.6 41.4 %copy-start.4 = (bf16[4,512,256]{2,1,0:T(8,128)(2,1)S(1)}, bf16[4,512,256]{2,1,0:T(8,128)(2,1)}, u32[]{:S(2)}) copy-start(bf16[4,512,256]{2,1,0:T(8,128)(2,1)} %leaf_u.3) | copy-start | bytes 3145732
  29.6 41.4 %copy-start.6 = (bf16[512,512]{1,0:T(8,128)(2,1)S(1)}, bf16[512,512]{1,0:T(8,128)(2,1)}, u32[]{:S(2)}) copy-start(bf16[512,512]{1,0:T(8,128)(2,1)} %root_cov_ref.1) | copy-start | bytes 1572868
  29.6 41.4 %copy-start.9 = (f32[512]{0:T(512)S(1)}, f32[512]{0:T(512)}, u32[]{:S(2)}) copy-start(f32[512]{0:T(512)} %param.29) | copy-start | bytes 6148
